TPU v7x, 256 devices: a whole 4x4x8 slice. The times are simulated.
256 devices in a mesh: frame: 32 (over x, y, core), head: 8 (over z).
Axes of the slice: x: 4, y: 4, z: 8, core: 2. Of those that a mesh axis runs over, the one named last changes fastest.
Arguments:
- queries: bfloat16 [1, 16384, 1024], P(None, 'frame', 'head'), may hold values from -256 to 256
- keys: bfloat16 [1, 16384, 1024], P(None, 'frame', 'head'), may hold values from -6 to 6
- values: bfloat16 [1, 16384, 1024], P(None, 'frame', 'head'), may hold values from -6 to 6
- out_weight: bfloat16 [1024, 1024], P('head'), may hold values from -0.1875 to 0.1875
- conv_kernel: bfloat16 [31, 1024], P(None, 'head'), may hold values from -1 to 1
- grad_out: bfloat16 [1024, 1, 16384], P('head', None, 'frame'), may hold values from -6 to 6
- pattern: int32 [1, 32, 7], replicated, may hold values from -1 to 31, as said below
- counts: int32 [1, 32], replicated, may hold values from 1 to 7, as said below
Outputs:
- conv_out: bfloat16 [1024, 1, 16384], P('head', None, 'frame')
- grad_queries: bfloat16 [1, 16384, 1024], P(None, 'frame', 'head')
- grad_keys: bfloat16 [1, 16384, 1024], P(None, 'frame', 'head')
- grad_values: bfloat16 [1, 16384, 1024], P(None, 'frame', 'head')
Inputs may be any that keep to these rules, and one draw needn't show every extreme that they name: pattern[s, b, 0] is b; the next entries are the blocks b + o with 0 < |o| <= 3 that lie inside the sequence, each once, in a drawn order; -1 fills the rest. counts[s, b] is at least 1 and at most the number of entries of row b that are not -1; in every sequence some block has 7.
All inputs are finite; a program needn't handle non-finite values.
Results may differ from a plain program's by a relative error of at most 0.035.
Values may be sent and summed in bfloat16 or wider, within the bound.
A program may use at most 64 MiB of HBM per device.

v0:
```python
from functools import partial
from functools import reduce

import jax
import jax.numpy as jnp
from jax import lax
from jax.sharding import PartitionSpec as P

HEAD_DIM = 64
KERNEL = 31
REACH = 3


NEGATIVE = -1e30


def from_behind(block, axis, distance):
    devices = range(lax.axis_size(axis))
    route = [(i - distance, i) for i in devices if i - distance in devices]
    return lax.ppermute(block, axis, route)


def with_halo(cells, sides, width):
    for axis, dim in sides:
        count = lax.axis_size(axis)
        ends = count - 1
        head = lax.slice_in_dim(cells, 0, width, axis=dim)
        tail = lax.slice_in_dim(cells, cells.shape[dim] - width, cells.shape[dim], axis=dim)
        cells = jnp.concatenate(
            [
                lax.ppermute(tail, axis, [(i, (i + 1) % count) for i in range(ends)]),
                cells,
                lax.ppermute(head, axis, [((i + 1) % count, i) for i in range(ends)]),
            ],
            axis=dim,
        )
    return cells


def reading(pattern, counts, query_block, key_block):
    blocks = pattern.shape[1]
    inside = (query_block >= 0) & (query_block < blocks) & (key_block >= 0) & (key_block < blocks)
    safe = jnp.clip(query_block, 0, blocks - 1)
    lists = lax.dynamic_index_in_dim(pattern, safe, 1, keepdims=False)
    number = lax.dynamic_index_in_dim(counts, safe, 1, keepdims=False)
    used = jnp.arange(lists.shape[1], dtype=jnp.int32)[None, :] < number[:, None]
    return inside & jnp.any((lists == key_block) & used, axis=1)


def masked_scores(query, key_part, allowed, scale):
    raw = jnp.einsum("sqhd,skhd->shqk", query, key_part, preferred_element_type=jnp.float32) * scale
    return jnp.where(allowed[:, None, None, None], raw, NEGATIVE)


def block_stats(query, key_part, allowed, scale):
    scores = masked_scores(query, key_part, allowed, scale)
    peak = jnp.max(scores, axis=3)
    return (peak, jnp.sum(jnp.exp(scores - peak[..., None]), axis=3))


def empty_stats(flat):
    return (jnp.full(flat, NEGATIVE, jnp.float32), jnp.zeros(flat, jnp.float32))


def keep_value(value):
    return value


def add_values(output, query, window, allowed, logsum, scale):
    scores = masked_scores(query, window[0], allowed, scale)
    weights = jnp.exp(scores - logsum[..., None]).astype(jnp.bfloat16)
    return output + jnp.einsum(
        "shqk,skhd->sqhd", weights, window[1], preferred_element_type=jnp.float32
    )


def back_parts(query, grad_heads, key_part, value_part, allowed, logsum, delta, scale):
    scores = masked_scores(query, key_part, allowed, scale)
    prob = jnp.exp(scores - logsum[..., None])
    slope = jnp.einsum(
        "sqhd,skhd->shqk", grad_heads, value_part, preferred_element_type=jnp.float32
    )
    grad_scores = (prob * (slope - delta[..., None]) * scale).astype(jnp.bfloat16)
    return (grad_scores, prob)


def key_terms(grad_scores, prob, query, grad_heads):
    grad_key = jnp.einsum("shqk,sqhd->skhd", grad_scores, query, preferred_element_type=jnp.float32)
    grad_value = jnp.einsum(
        "shqk,sqhd->skhd", prob.astype(jnp.bfloat16), grad_heads, preferred_element_type=jnp.float32
    )
    seq_count, row_count = (grad_key.shape[0], grad_key.shape[1])
    return jnp.concatenate(
        [grad_key.reshape(seq_count, row_count, -1), grad_value.reshape(seq_count, row_count, -1)],
        axis=2,
    )


def back_full(grad_q, query, grad_heads, window, allowed, logsum, delta, scale):
    grad_scores, prob = back_parts(
        query, grad_heads, window[0], window[1], allowed, logsum, delta, scale
    )
    grad_q = grad_q + jnp.einsum(
        "shqk,skhd->sqhd", grad_scores, window[0], preferred_element_type=jnp.float32
    )
    return (grad_q, key_terms(grad_scores, prob, query, grad_heads))


def skip_full(grad_q, blank):
    return (grad_q, blank)


def on_device(queries, keys, values, out_weight, conv_kernel, grad_out, pattern, counts):
    seqs, rows, width = queries.shape
    heads = width // HEAD_DIM
    scale = HEAD_DIM ** (-0.5)
    split = (seqs, rows, heads, HEAD_DIM)
    flat = (seqs, heads, rows)
    here = lax.axis_index("frame")
    offsets = list(range(-REACH, REACH + 1))
    query_heads = queries.reshape(split)
    both = jnp.concatenate([keys, values], axis=2)
    windows = []
    allowed = []
    for step in offsets:
        if step == 0:
            block = both
        else:
            block = from_behind(both, "frame", -step)
        windows.append((block[:, :, :width].reshape(split), block[:, :, width:].reshape(split)))
        allowed.append(reading(pattern, counts, here, here + step))
    partials = []
    for index in range(len(offsets)):
        partials.append(
            lax.cond(
                jnp.any(allowed[index]),
                partial(block_stats, query_heads, windows[index][0], allowed[index], scale),
                partial(empty_stats, flat),
            )
        )
    peak = reduce(jnp.maximum, [item[0] for item in partials])
    total = reduce(jnp.add, [item[1] * jnp.exp(item[0] - peak) for item in partials])
    logsum = peak + jnp.log(total)
    output = jnp.zeros(split, jnp.float32)
    for index in range(len(offsets)):
        output = lax.cond(
            jnp.any(allowed[index]),
            partial(add_values, output, query_heads, windows[index], allowed[index], logsum, scale),
            partial(keep_value, output),
        )
    attended = output.reshape(seqs, rows, width).astype(jnp.bfloat16)
    channels = out_weight.shape[1] // lax.axis_size("head")
    part = out_weight
    mixed = lax.psum_scatter(
        jnp.einsum("ac,sra->csr", part, attended, preferred_element_type=jnp.float32),
        "head",
        scatter_dimension=0,
        tiled=True,
    ).astype(jnp.bfloat16)
    stacked = jnp.concatenate([mixed, grad_out], axis=0)
    half = KERNEL // 2
    rims = with_halo(stacked, (("frame", 2),), half)
    taps = conv_kernel.astype(jnp.float32)
    forward_sum = jnp.zeros((channels, seqs, rows), jnp.float32)
    reverse_sum = jnp.zeros((channels, seqs, rows), jnp.float32)
    for tap in range(KERNEL):
        weight = taps[tap][:, None, None]
        forward_sum = forward_sum + weight * rims[:channels, :, tap : tap + rows]
        reverse_sum = (
            reverse_sum + weight * rims[channels:, :, 2 * half - tap : 2 * half - tap + rows]
        )
    conv_out = forward_sum.astype(jnp.bfloat16)
    grad_mixed = reverse_sum.astype(jnp.bfloat16)
    part = out_weight
    grad_attended = jnp.einsum(
        "csr,ac->sra",
        lax.all_gather(grad_mixed, "head", axis=0, tiled=True),
        part,
        preferred_element_type=jnp.float32,
    ).astype(jnp.bfloat16)
    grad_heads = grad_attended.reshape(split)
    delta = jnp.transpose(
        jnp.sum(
            grad_heads.astype(jnp.float32) * attended.reshape(split).astype(jnp.float32), axis=3
        ),
        (0, 2, 1),
    )
    grad_q = jnp.zeros(split, jnp.float32)
    blank = jnp.zeros((seqs, rows, 2 * width), jnp.float32)
    key_grad = blank
    for index, step in enumerate(offsets):
        grad_q, term = lax.cond(
            jnp.any(allowed[index]),
            partial(
                back_full,
                grad_q,
                query_heads,
                grad_heads,
                windows[index],
                allowed[index],
                logsum,
                delta,
                scale,
            ),
            partial(skip_full, grad_q, blank),
        )
        if step == 0:
            arrived = term
        else:
            arrived = from_behind(term.astype(jnp.bfloat16), "frame", step).astype(term.dtype)
        key_grad = key_grad + arrived
    grad_queries = grad_q.reshape(seqs, rows, width).astype(jnp.bfloat16)
    grad_keys = key_grad[:, :, :width].astype(jnp.bfloat16)
    grad_values = key_grad[:, :, width:].astype(jnp.bfloat16)
    return (conv_out, grad_queries, grad_keys, grad_values)


def solution(mesh):
    return jax.shard_map(
        on_device,
        mesh=mesh,
        in_specs=(
            P(None, "frame", "head"),
            P(None, "frame", "head"),
            P(None, "frame", "head"),
            P("head", None),
            P(None, "head"),
            P("head", None, "frame"),
            P(),
            P(),
        ),
        out_specs=(
            P("head", None, "frame"),
            P(None, "frame", "head"),
            P(None, "frame", "head"),
            P(None, "frame", "head"),
        ),
        check_vma=False,
    )
```

profile of v0, /device:TPU:21, one launch (start us, length us, event | category | flops | bytes accessed | tf_op | source)
XLA Modules:
  0.0 238.5 jit_solution(12214543152311739085)
XLA Ops:
  9.1 2.6 %collective-permute-start.5 = (bf16[1,512,256]{2,1,0:T(8,128)(2,1)S(1)}, bf16[1,512,256]{2,1,0:T(8,128)(2,1)S(1)}, u32[]{:S(2)}, u32[]{:S(2)}) collective-permute-start(bf16[1,512,256]{2,1,0:T(8,128)(2,1)S(1)} %constant_dynamic-update-slice_fusion), channel_id=1, source_target_pairs={{24,0},{32,8},{40,16},{48,24},{56,32},{64,40},{72,48},{80,56},{88,... | collective-permute-start | bytes 786440 | tf_op jit(solution)/shard_map/ppermute | solution.py:20
  11.8 2.1 collective-permute-start.4
  13.9 3.8 %collective-permute-start.3 = (bf16[1,512,256]{2,1,0:T(8,128)(2,1)S(1)}, bf16[1,512,256]{2,1,0:T(8,128)(2,1)S(1)}, u32[]{:S(2)}, u32[]{:S(2)}) collective-permute-start(bf16[1,512,256]{2,1,0:T(8,128)(2,1)S(1)} %constant_dynamic-update-slice_fusion), channel_id=1, source_target_pairs={{8,0},{16,8},{24,16},{32,24},{40,32},{48,40},{56,48},{64,56},{72,6... | collective-permute-start | bytes 786440 | tf_op jit(solution)/shard_map/ppermute | solution.py:20
  17.7 1.9 collective-permute-start.2
  19.6 5.2 %collective-permute-start.1 = (bf16[1,512,256]{2,1,0:T(8,128)(2,1)S(1)}, bf16[1,512,256]{2,1,0:T(8,128)(2,1)S(1)}, u32[]{:S(2)}, u32[]{:S(2)}) collective-permute-start(bf16[1,512,256]{2,1,0:T(8,128)(2,1)S(1)} %constant_dynamic-update-slice_fusion), channel_id=1, source_target_pairs={{0,16},{8,24},{16,32},{24,40},{32,48},{40,56},{48,64},{56,72},{64,... | collective-permute-start | bytes 786440 | tf_op jit(solution)/shard_map/ppermute | solution.py:20
  40.6 2.2 conditional.24
  42.8 2.6 %collective-permute-start = (bf16[1,512,256]{2,1,0:T(8,128)(2,1)S(1)}, bf16[1,512,256]{2,1,0:T(8,128)(2,1)S(1)}, u32[]{:S(2)}, u32[]{:S(2)}) collective-permute-start(bf16[1,512,256]{2,1,0:T(8,128)(2,1)S(1)} %constant_dynamic-update-slice_fusion), channel_id=1, source_target_pairs={{0,24},{8,32},{16,40},{24,48},{32,56},{40,64},{48,72},{56,80},{64,... | collective-permute-start | bytes 786440 | tf_op jit(solution)/shard_map/ppermute | solution.py:20
  46.8 5.8 %collective-permute-done = bf16[1,512,256]{2,1,0:T(8,128)(2,1)S(1)} collective-permute-done((bf16[1,512,256]{2,1,0:T(8,128)(2,1)S(1)}, bf16[1,512,256]{2,1,0:T(8,128)(2,1)S(1)}, u32[]{:S(2)}, u32[]{:S(2)}) %collective-permute-start) | collective-permute-done | bytes 262176 | tf_op jit(solution)/shard_map/ppermute | solution.py:20
  52.8 2.2 conditional.27
  55.1 2.2 conditional.26
  57.3 2.2 conditional.25
  59.5 2.2 conditional.23
  61.7 2.2 conditional.22
  63.9 2.2 conditional.21
  75.7 40.2 %reduce-scatter.2.cloned.1.call-done = f32[128,1,512]{0,2,1:T(8,128)} async-done(((f32[1024,1,512]{0,2,1:T(8,128)}), f32[128,1,512]{0,2,1:T(8,128)}) %reduce-scatter.2.cloned.1.call-update) | async-done | bytes 262160 | tf_op jit(solution)/shard_map/reduce_scatter | solution.py:154
  117.0 7.5 %collective-permute-start.6 = (bf16[256,1,15]{0,2,1:T(8,128)(2,1)S(1)}, bf16[256,1,15]{0,2,1:T(8,128)(2,1)S(1)}, u32[]{:S(2)}, u32[]{:S(2)}) collective-permute-start(bf16[256,1,15]{0,2,1:T(8,128)(2,1)S(1)} %get-tuple-element.560), channel_id=1, source_target_pairs={{0,8},{8,16},{16,24},{24,32},{32,40},{40,48},{48,56},{56,64},{64,7... | collective-permute-start | bytes 23048 | tf_op jit(solution)/shard_map/ppermute | solution.py:31
  124.5 1.9 collective-permute-start.7
  126.6 2.9 %collective-permute-done.7 = bf16[256,1,15]{0,2,1:T(8,128)(2,1)S(1)} collective-permute-done((bf16[256,1,15]{0,2,1:T(8,128)(2,1)S(1)}, bf16[256,1,15]{0,2,1:T(8,128)(2,1)S(1)}, u32[]{:S(2)}, u32[]{:S(2)}) %collective-permute-start.7) | collective-permute-done | bytes 7712 | tf_op jit(solution)/shard_map/ppermute | solution.py:33
  131.7 35.7 %all-gather.2.cloned.1.call-done = bf16[1024,1,512]{0,2,1:T(8,128)(2,1)} async-done(((bf16[128,1,512]{0,2,1:T(8,128)(2,1)}), bf16[1024,1,512]{0,2,1:T(8,128)(2,1)}) %all-gather.2.cloned.1.call-update) | async-done | bytes 1048592 | tf_op jit(solution)/shard_map/all_gather | solution.py:177
  169.1 2.2 conditional.35
  171.3 2.2 conditional.36
  174.2 2.2 conditional.37
  177.1 2.4 %conditional.38 = (f32[1,512,2,64]{1,3,2,0:T(8,128)S(1)}, f32[1,512,256]{2,1,0:T(8,128)S(1)}) conditional(s32[]{:T(128)} %convert_element_type.411, f32[1,512,2,64]{1,3,2,0:T(8,128)S(1)} %get-tuple-element.432, (pred[1]{0:T(512)(128)(4,1)}, bf16[1,512,2,64]{1,3,2,0:T(8,128)(2,1)S(1)}, bf16[1,512,2,64]{1,3,2,0:T(8,128)(2,1)S(1)}, ...), branch_computations={%region_57.58_spmd, %region_58.59_spmd} | conditional | flops 339935232 | bytes 13508625 | solution.py:192
  179.5 2.5 %conditional.39 = (f32[1,512,2,64]{1,3,2,0:T(8,128)S(1)}, bf16[1,512,256]{1,2,0:T(8,128)(2,1)S(1)}) conditional(s32[]{:T(128)} %convert_element_type.410, f32[1,512,2,64]{1,3,2,0:T(8,128)S(1)} %get-tuple-element.433, (pred[1]{0:T(512)(128)(4,1)}, bf16[1,512,2,64]{1,3,2,0:T(8,128)(2,1)S(1)}, bf16[1,512,2,64]{1,3,2,0:T(8,128)(2,1)S(1)}, ...), branch_computations={%region_59.60_spmd, %region_60.61_spmd} | conditional | flops 340328448 | bytes 12197933 | solution.py:192
  182.0 2.2 conditional.40
  185.0 2.9 %conditional.41 = (f32[1,512,2,64]{1,3,2,0:T(8,128)S(1)}, bf16[1,512,256]{1,2,0:T(8,128)(2,1)}) conditional(s32[]{:T(128)} %convert_element_type.408, f32[1,512,2,64]{1,3,2,0:T(8,128)S(1)} %get-tuple-element.435, (pred[1]{0:T(512)(128)(4,1)}, bf16[1,512,2,64]{1,3,2,0:T(8,128)(2,1)S(1)}, bf16[1,512,2,64]{1,3,2,0:T(8,128)(2,1)S(1)}, ...), branch_computations={%region_63.64_spmd, %region_64.65_spmd} | conditional | flops 340328448 | bytes 11673617 | solution.py:192
  189.7 5.8 %collective-permute-start.13 = (bf16[1,512,256]{2,1,0:T(8,128)(2,1)}, bf16[1,512,256]{2,1,0:T(8,128)(2,1)S(1)}, u32[]{:S(2)}, u32[]{:S(2)}) collective-permute-start(bf16[1,512,256]{2,1,0:T(8,128)(2,1)} %copy.89), channel_id=1, source_target_pairs={{0,24},{8,32},{16,40},{24,48},{32,56},{40,64},{48,72},{56,80},{64,... | collective-permute-start | bytes 786440 | tf_op jit(solution)/shard_map/ppermute | solution.py:20
  199.8 5.3 %collective-permute-start.12 = (bf16[1,512,256]{2,1,0:T(8,128)(2,1)}, bf16[1,512,256]{2,1,0:T(8,128)(2,1)S(1)}, u32[]{:S(2)}, u32[]{:S(2)}) collective-permute-start(bf16[1,512,256]{2,1,0:T(8,128)(2,1)} %copy.88), channel_id=1, source_target_pairs={{0,16},{8,24},{16,32},{24,40},{32,48},{40,56},{48,64},{56,72},{64,... | collective-permute-start | bytes 786440 | tf_op jit(solution)/shard_map/ppermute | solution.py:20
  205.1 1.9 collective-permute-start.11
  207.0 2.4 %collective-permute-start.10 = (bf16[1,512,256]{2,1,0:T(8,128)(2,1)}, bf16[1,512,256]{2,1,0:T(8,128)(2,1)S(1)}, u32[]{:S(2)}, u32[]{:S(2)}) collective-permute-start(bf16[1,512,256]{2,1,0:T(8,128)(2,1)} %copy.85), channel_id=1, source_target_pairs={{8,0},{16,8},{24,16},{32,24},{40,32},{48,40},{56,48},{64,56},{72,6... | collective-permute-start | bytes 786440 | tf_op jit(solution)/shard_map/ppermute | solution.py:20
  211.4 3.4 %collective-permute-start.8 = (bf16[1,512,256]{2,1,0:T(8,128)(2,1)}, bf16[1,512,256]{2,1,0:T(8,128)(2,1)S(1)}, u32[]{:S(2)}, u32[]{:S(2)}) collective-permute-start(bf16[1,512,256]{2,1,0:T(8,128)(2,1)} %copy.83), channel_id=1, source_target_pairs={{24,0},{32,8},{40,16},{48,24},{56,32},{64,40},{72,48},{80,56},{88,... | collective-permute-start | bytes 786440 | tf_op jit(solution)/shard_map/ppermute | solution.py:20
  219.9 10.8 %collective-permute-done.8 = bf16[1,512,256]{2,1,0:T(8,128)(2,1)S(1)} collective-permute-done((bf16[1,512,256]{2,1,0:T(8,128)(2,1)}, bf16[1,512,256]{2,1,0:T(8,128)(2,1)S(1)}, u32[]{:S(2)}, u32[]{:S(2)}) %collective-permute-start.8) | collective-permute-done | bytes 262176 | tf_op jit(solution)/shard_map/ppermute | solution.py:20
  (235 shorter events, 82.3 us)
Async XLA Ops:
  7.2 66.3 %copy-start = (bf16[128,1024]{1,0:T(8,128)(2,1)S(1)}, bf16[128,1024]{1,0:T(8,128)(2,1)}, u32[]{:S(2)}) copy-start(bf16[128,1024]{1,0:T(8,128)(2,1)} %param.53) | copy-start | bytes 786436
  7.2 108.8 %reduce-scatter.2.cloned.1.call-start = ((), (), s32[]{:S(2)}) async-start(), calls=%async_computation.1 | async-start | bytes 2359296 | tf_op jit(solution)/shard_map/reduce_scatter | solution.py:154
  9.1 33.7 %collective-permute-start.5 = (bf16[1,512,256]{2,1,0:T(8,128)(2,1)S(1)}, bf16[1,512,256]{2,1,0:T(8,128)(2,1)S(1)}, u32[]{:S(2)}, u32[]{:S(2)}) collective-permute-start(bf16[1,512,256]{2,1,0:T(8,128)(2,1)S(1)} %constant_dynamic-update-slice_fusion), channel_id=1, source_target_pairs={{24,0},{32,8},{40,16},{48,24},{56,32},{64,40},{72,48},{80,56},{88,... | collective-permute-start | bytes 786440 | tf_op jit(solution)/shard_map/ppermute | solution.py:20
  11.8 33.6 %collective-permute-start.4 = (bf16[1,512,256]{2,1,0:T(8,128)(2,1)S(1)}, bf16[1,512,256]{2,1,0:T(8,128)(2,1)S(1)}, u32[]{:S(2)}, u32[]{:S(2)}) collective-permute-start(bf16[1,512,256]{2,1,0:T(8,128)(2,1)S(1)} %constant_dynamic-update-slice_fusion), channel_id=1, source_target_pairs={{16,0},{24,8},{32,16},{40,24},{48,32},{56,40},{64,48},{72,56},{80,... | collective-permute-start | bytes 786440 | tf_op jit(solution)/shard_map/ppermute | solution.py:20
  13.9 31.6 %collective-permute-start.3 = (bf16[1,512,256]{2,1,0:T(8,128)(2,1)S(1)}, bf16[1,512,256]{2,1,0:T(8,128)(2,1)S(1)}, u32[]{:S(2)}, u32[]{:S(2)}) collective-permute-start(bf16[1,512,256]{2,1,0:T(8,128)(2,1)S(1)} %constant_dynamic-update-slice_fusion), channel_id=1, source_target_pairs={{8,0},{16,8},{24,16},{32,24},{40,32},{48,40},{56,48},{64,56},{72,6... | collective-permute-start | bytes 786440 | tf_op jit(solution)/shard_map/ppermute | solution.py:20
  17.7 27.8 %collective-permute-start.2 = (bf16[1,512,256]{2,1,0:T(8,128)(2,1)S(1)}, bf16[1,512,256]{2,1,0:T(8,128)(2,1)S(1)}, u32[]{:S(2)}, u32[]{:S(2)}) collective-permute-start(bf16[1,512,256]{2,1,0:T(8,128)(2,1)S(1)} %constant_dynamic-update-slice_fusion), channel_id=1, source_target_pairs={{0,8},{8,16},{16,24},{24,32},{32,40},{40,48},{48,56},{56,64},{64,7... | collective-permute-start | bytes 786440 | tf_op jit(solution)/shard_map/ppermute | solution.py:20
  19.6 26.9 %collective-permute-start.1 = (bf16[1,512,256]{2,1,0:T(8,128)(2,1)S(1)}, bf16[1,512,256]{2,1,0:T(8,128)(2,1)S(1)}, u32[]{:S(2)}, u32[]{:S(2)}) collective-permute-start(bf16[1,512,256]{2,1,0:T(8,128)(2,1)S(1)} %constant_dynamic-update-slice_fusion), channel_id=1, source_target_pairs={{0,16},{8,24},{16,32},{24,40},{32,48},{40,56},{48,64},{56,72},{64,... | collective-permute-start | bytes 786440 | tf_op jit(solution)/shard_map/ppermute | solution.py:20
  42.8 9.7 %collective-permute-start = (bf16[1,512,256]{2,1,0:T(8,128)(2,1)S(1)}, bf16[1,512,256]{2,1,0:T(8,128)(2,1)S(1)}, u32[]{:S(2)}, u32[]{:S(2)}) collective-permute-start(bf16[1,512,256]{2,1,0:T(8,128)(2,1)S(1)} %constant_dynamic-update-slice_fusion), channel_id=1, source_target_pairs={{0,24},{8,32},{16,40},{24,48},{32,56},{40,64},{48,72},{56,80},{64,... | collective-permute-start | bytes 786440 | tf_op jit(solution)/shard_map/ppermute | solution.py:20
  75.3 92.0 %all-gather.2.cloned.1.call-start = ((), (), s32[]{:S(2)}) async-start(), calls=%async_computation.2 | async-start | bytes 1179648 | tf_op jit(solution)/shard_map/all_gather | solution.py:177
  75.6 55.9 %copy-start.16 = (f32[128]{0:T(128)}, f32[128]{0:T(128)S(1)}, u32[]{:S(2)}) copy-start(f32[128]{0:T(128)S(1)} %get-tuple-element.574) | copy-start | bytes 1540
  75.6 55.9 %copy-start.17 = (f32[128]{0:T(128)}, f32[128]{0:T(128)S(1)}, u32[]{:S(2)}) copy-start(f32[128]{0:T(128)S(1)} %get-tuple-element.575) | copy-start | bytes 1540
  75.6 55.9 %copy-start.18 = (f32[128]{0:T(128)}, f32[128]{0:T(128)S(1)}, u32[]{:S(2)}) copy-start(f32[128]{0:T(128)S(1)} %get-tuple-element.576) | copy-start | bytes 1540
  75.6 55.9 %copy-start.19 = (f32[128]{0:T(128)}, f32[128]{0:T(128)S(1)}, u32[]{:S(2)}) copy-start(f32[128]{0:T(128)S(1)} %get-tuple-element.577) | copy-start | bytes 1540
  75.6 55.9 %copy-start.20 = (f32[128]{0:T(128)}, f32[128]{0:T(128)S(1)}, u32[]{:S(2)}) copy-start(f32[128]{0:T(128)S(1)} %get-tuple-element.578) | copy-start | bytes 1540
  75.6 55.9 %copy-start.21 = (f32[128]{0:T(128)}, f32[128]{0:T(128)S(1)}, u32[]{:S(2)}) copy-start(f32[128]{0:T(128)S(1)} %get-tuple-element.579) | copy-start | bytes 1540
  75.6 55.9 %copy-start.22 = (f32[128]{0:T(128)}, f32[128]{0:T(128)S(1)}, u32[]{:S(2)}) copy-start(f32[128]{0:T(128)S(1)} %get-tuple-element.580) | copy-start | bytes 1540
  75.6 55.9 %copy-start.23 = (f32[128]{0:T(128)}, f32[128]{0:T(128)S(1)}, u32[]{:S(2)}) copy-start(f32[128]{0:T(128)S(1)} %get-tuple-element.581) | copy-start | bytes 1540
  75.6 55.9 %copy-start.24 = (f32[128]{0:T(128)}, f32[128]{0:T(128)S(1)}, u32[]{:S(2)}) copy-start(f32[128]{0:T(128)S(1)} %get-tuple-element.582) | copy-start | bytes 1540
  75.6 55.9 %copy-start.25 = (f32[128]{0:T(128)}, f32[128]{0:T(128)S(1)}, u32[]{:S(2)}) copy-start(f32[128]{0:T(128)S(1)} %get-tuple-element.583) | copy-start | bytes 1540
  75.7 55.9 %copy-start.26 = (f32[128]{0:T(128)}, f32[128]{0:T(128)S(1)}, u32[]{:S(2)}) copy-start(f32[128]{0:T(128)S(1)} %get-tuple-element.584) | copy-start | bytes 1540
  75.7 55.9 %copy-start.27 = (f32[128]{0:T(128)}, f32[128]{0:T(128)S(1)}, u32[]{:S(2)}) copy-start(f32[128]{0:T(128)S(1)} %get-tuple-element.585) | copy-start | bytes 1540
  75.7 55.9 %copy-start.28 = (f32[128]{0:T(128)}, f32[128]{0:T(128)S(1)}, u32[]{:S(2)}) copy-start(f32[128]{0:T(128)S(1)} %get-tuple-element.586) | copy-start | bytes 1540
  75.7 55.9 %copy-start.29 = (f32[128]{0:T(128)}, f32[128]{0:T(128)S(1)}, u32[]{:S(2)}) copy-start(f32[128]{0:T(128)S(1)} %get-tuple-element.587) | copy-start | bytes 1540
  75.7 55.9 %copy-start.30 = (f32[128]{0:T(128)}, f32[128]{0:T(128)S(1)}, u32[]{:S(2)}) copy-start(f32[128]{0:T(128)S(1)} %get-tuple-element.588) | copy-start | bytes 1540
  117.0 9.6 %collective-permute-start.6 = (bf16[256,1,15]{0,2,1:T(8,128)(2,1)S(1)}, bf16[256,1,15]{0,2,1:T(8,128)(2,1)S(1)}, u32[]{:S(2)}, u32[]{:S(2)}) collective-permute-start(bf16[256,1,15]{0,2,1:T(8,128)(2,1)S(1)} %get-tuple-element.560), channel_id=1, source_target_pairs={{0,8},{8,16},{16,24},{24,32},{32,40},{40,48},{48,56},{56,64},{64,7... | collective-permute-start | bytes 23048 | tf_op jit(solution)/shard_map/ppermute | solution.py:31
  124.5 5.0 %collective-permute-start.7 = (bf16[256,1,15]{0,2,1:T(8,128)(2,1)S(1)}, bf16[256,1,15]{0,2,1:T(8,128)(2,1)S(1)}, u32[]{:S(2)}, u32[]{:S(2)}) collective-permute-start(bf16[256,1,15]{0,2,1:T(8,128)(2,1)S(1)} %get-tuple-element.561), channel_id=1, source_target_pairs={{8,0},{16,8},{24,16},{32,24},{40,32},{48,40},{56,48},{64,56},{72,6... | collective-permute-start | bytes 23048 | tf_op jit(solution)/shard_map/ppermute | solution.py:33
  189.7 21.6 %collective-permute-start.13 = (bf16[1,512,256]{2,1,0:T(8,128)(2,1)}, bf16[1,512,256]{2,1,0:T(8,128)(2,1)S(1)}, u32[]{:S(2)}, u32[]{:S(2)}) collective-permute-start(bf16[1,512,256]{2,1,0:T(8,128)(2,1)} %copy.89), channel_id=1, source_target_pairs={{0,24},{8,32},{16,40},{24,48},{32,56},{40,64},{48,72},{56,80},{64,... | collective-permute-start | bytes 786440 | tf_op jit(solution)/shard_map/ppermute | solution.py:20
  199.8 18.4 %collective-permute-start.12 = (bf16[1,512,256]{2,1,0:T(8,128)(2,1)}, bf16[1,512,256]{2,1,0:T(8,128)(2,1)S(1)}, u32[]{:S(2)}, u32[]{:S(2)}) collective-permute-start(bf16[1,512,256]{2,1,0:T(8,128)(2,1)} %copy.88), channel_id=1, source_target_pairs={{0,16},{8,24},{16,32},{24,40},{32,48},{40,56},{48,64},{56,72},{64,... | collective-permute-start | bytes 786440 | tf_op jit(solution)/shard_map/ppermute | solution.py:20
  205.1 13.1 %collective-permute-start.11 = (bf16[1,512,256]{2,1,0:T(8,128)(2,1)}, bf16[1,512,256]{2,1,0:T(8,128)(2,1)S(1)}, u32[]{:S(2)}, u32[]{:S(2)}) collective-permute-start(bf16[1,512,256]{2,1,0:T(8,128)(2,1)} %copy.87), channel_id=1, source_target_pairs={{0,8},{8,16},{16,24},{24,32},{32,40},{40,48},{48,56},{56,64},{64,7... | collective-permute-start | bytes 786440 | tf_op jit(solution)/shard_map/ppermute | solution.py:20
  207.0 11.1 %collective-permute-start.10 = (bf16[1,512,256]{2,1,0:T(8,128)(2,1)}, bf16[1,512,256]{2,1,0:T(8,128)(2,1)S(1)}, u32[]{:S(2)}, u32[]{:S(2)}) collective-permute-start(bf16[1,512,256]{2,1,0:T(8,128)(2,1)} %copy.85), channel_id=1, source_target_pairs={{8,0},{16,8},{24,16},{32,24},{40,32},{48,40},{56,48},{64,56},{72,6... | collective-permute-start | bytes 786440 | tf_op jit(solution)/shard_map/ppermute | solution.py:20
  209.4 10.5 %collective-permute-start.9 = (bf16[1,512,256]{2,1,0:T(8,128)(2,1)}, bf16[1,512,256]{2,1,0:T(8,128)(2,1)S(1)}, u32[]{:S(2)}, u32[]{:S(2)}) collective-permute-start(bf16[1,512,256]{2,1,0:T(8,128)(2,1)} %copy.84), channel_id=1, source_target_pairs={{16,0},{24,8},{32,16},{40,24},{48,32},{56,40},{64,48},{72,56},{80,... | collective-permute-start | bytes 786440 | tf_op jit(solution)/shard_map/ppermute | solution.py:20
  211.4 19.3 %collective-permute-start.8 = (bf16[1,512,256]{2,1,0:T(8,128)(2,1)}, bf16[1,512,256]{2,1,0:T(8,128)(2,1)S(1)}, u32[]{:S(2)}, u32[]{:S(2)}) collective-permute-start(bf16[1,512,256]{2,1,0:T(8,128)(2,1)} %copy.83), channel_id=1, source_target_pairs={{24,0},{32,8},{40,16},{48,24},{56,32},{64,40},{72,48},{80,56},{88,... | collective-permute-start | bytes 786440 | tf_op jit(solution)/shard_map/ppermute | solution.py:20
  (31 other events, 412.3 us)
Sparse Core Ops, SparseCore 0:
  75.4 40.4 reduce-scatter.1
  131.8 35.4 all-gather.1
where the time goes:
time: 240 us; the launch traced here: 238 us
  waiting for transfers between devices  97.1 us (40%)
  starting transfers between devices  48.5 us (20%)
  matrix products  32.2 us (13%)
  other arithmetic  21.3 us (9%)
  between operations  19.7 us (8%)
  local copies, waits for them, and re-layouts  18.5 us (8%)
    reduce_scatter x1, waiting for transfers between devices, on_device(): lax.psum_scatter(jnp.einsum('ac,sra->csr', part, attended, preferred_elem...  40.2 us
    ppermute x12, starting transfers between devices, from_behind(): return lax.ppermute(block, axis, route)  39 us
    all_gather x1, waiting for transfers between devices, on_device(): lax.all_gather(grad_mixed, 'head', axis=0, tiled=True)  35.7 us
    ppermute x12, waiting for transfers between devices, from_behind(): return lax.ppermute(block, axis, route)  18.3 us
    dot_general x14, matrix products, masked_scores(): jnp.einsum('sqhd,skhd->shqk', query, key_part, preferred_element_type=jnp...  11.8 us
    unnamed x99, local copies, waits for them, and re-layouts  7.9 us
    reduce_sum x7, other arithmetic, block_stats(): return (peak, jnp.sum(jnp.exp(scores - peak[..., None]), axis=3))  7.73 us
    ppermute x1, starting transfers between devices, with_halo(): lax.ppermute(tail, axis, [(i, (i + 1) % count) for i in range(ends)])  7.53 us
  transfers between devices with their start and end apart: 16, of which 6 were waited for; matrix products, arithmetic and copies ran while one was open for 9% of the time, Pallas kernels for 0%

commit v1 on v0

v1 whole, which is shorter than its diff:
```python
from functools import partial

import jax
import jax.numpy as jnp
from jax import lax
from jax.experimental import pallas as pl
from jax.experimental.pallas import tpu as pltpu
from jax.sharding import PartitionSpec as P

HEAD_DIM = 64
KERNEL = 31
REACH = 3
SPAN = 2 * REACH + 1
HUGE = 1e30
MESH = pl.DeviceIdType.MESH
ORDER = (0, 1, -1, 2, -2, 3, -3)
NEIGHBOURS = (1, -1, 2, -2, 3, -3)
RIM = 16

NT = (((1,), (1,)), ((), ()))
NN = (((1,), (0,)), ((), ()))


def dot(a, b, dims):
    return lax.dot_general(a, b, dims, preferred_element_type=jnp.float32)


def kernel(
    frames,
    heads,
    q_ref,
    k_ref,
    v_ref,
    w_ref,
    t_ref,
    g_ref,
    pat_ref,
    cnt_ref,
    co_ref,
    dq_ref,
    dk_ref,
    dv_ref,
    kv,
    qs,
    do,
    stats,
    gm_all,
    at_all,
    wcol,
    go_t,
    mixed,
    halo,
    pad,
    taps,
    qm,
    km,
    vm,
    dom,
    probs,
    peaks,
    peak,
    total,
    acc,
    delta,
    acc2,
    kv_s,
    kv_r,
    q_s,
    q_r,
    do_s,
    do_r,
    st_s,
    st_r,
    w_s,
    w_r,
    gm_s,
    gm_r,
    at_s,
    at_r,
    h_s,
    h_r,
):
    f = lax.axis_index("frame")
    z = lax.axis_index("head")
    rows, width = q_ref.shape
    R = 256

    def fdev(o):
        return (lax.rem(f + o + frames, frames), z)

    def zrel(i):
        return lax.rem(z + i, heads)

    def remote(src, dst, s, r, dev):
        return pltpu.make_async_remote_copy(
            src_ref=src, dst_ref=dst, send_sem=s, recv_sem=r, device_id=dev, device_id_type=MESH
        )

    barrier = pltpu.get_barrier_semaphore()
    for o in NEIGHBOURS:
        pl.semaphore_signal(barrier, inc=1, device_id=fdev(o), device_id_type=MESH)
    for i in range(1, heads):
        pl.semaphore_signal(barrier, inc=1, device_id=(f, zrel(i)), device_id_type=MESH)

    lane = lax.broadcasted_iota(jnp.int32, (rows, width), 1)
    low = lane < HEAD_DIM

    def split_heads(x, dst):
        x = x.astype(jnp.float32)
        dst[0:rows, :] = jnp.where(low, x, 0.0).astype(jnp.bfloat16)
        dst[rows : 2 * rows, :] = jnp.where(low, 0.0, x).astype(jnp.bfloat16)

    kv[REACH, 0] = k_ref[...]
    kv[REACH, 1] = v_ref[...]
    scaled = (q_ref[...].astype(jnp.float32) * HEAD_DIM**-0.5).astype(jnp.bfloat16)
    qs[REACH] = scaled
    go_t[...] = g_ref[...].T
    taps[0:KERNEL, :] = t_ref[...].astype(jnp.float32)

    pl.semaphore_wait(barrier, len(NEIGHBOURS) + heads - 1)

    def shift(buf, s, r, o):
        return remote(buf.at[REACH], buf.at[REACH - o], s.at[REACH - o], r.at[REACH - o], fdev(o))

    def edge(buf, which, o):
        src = buf.at[pl.ds(rows - RIM, RIM)] if o == 1 else buf.at[pl.ds(0, RIM)]
        side = 0 if o == 1 else 1
        return remote(src, halo.at[which, side], h_s.at[which, side], h_r.at[which, side], fdev(o))

    def spread(buf, s, r, i):
        return remote(buf.at[z], buf.at[z], s.at[i], r.at[z], (f, zrel(i)))

    def spread_arrived(buf, s, r, i):
        src = zrel(i)
        return remote(buf.at[src], buf.at[src], s.at[i], r.at[src], (f, src))

    def weight(i):
        there = zrel(i)
        cols = pl.ds(pl.multiple_of(there * width, width), width)
        return remote(w_ref.at[:, cols], wcol.at[z], w_s.at[i], w_r.at[z], (f, there))

    for o in (1, -1):
        edge(go_t, 0, o).start()
    for o in NEIGHBOURS:
        shift(kv, kv_s, kv_r, o).start()
    for i in range(1, heads):
        weight(i).start()
    for o in NEIGHBOURS:
        shift(qs, q_s, q_r, o).start()
    own_cols = pl.ds(pl.multiple_of(z * width, width), width)
    wcol[z] = w_ref[:, own_cols]

    split_heads(qs[REACH], qm)
    split_heads(k_ref[...], km)
    split_heads(v_ref[...], vm)

    def conv(src, which, flip, out):
        for o in (1, -1):
            edge(src, which, o).wait_recv()
        left = halo[which, 0].astype(jnp.float32)
        right = halo[which, 1].astype(jnp.float32)
        pad[0:RIM, :] = jnp.where(f > 0, left, 0.0)
        pad[RIM : RIM + rows, :] = src[...].astype(jnp.float32)
        pad[RIM + rows : 2 * RIM + rows, :] = jnp.where(f < frames - 1, right, 0.0)
        step = 64
        for c in range(rows // step):
            total_c = jnp.zeros((step, width), jnp.float32)
            for t in range(KERNEL):
                tap = KERNEL - 1 - t if flip else t
                total_c = total_c + taps[tap : tap + 1, :] * pad[c * step + t + 1 : c * step + t + 1 + step, :]
            out(c * step, step, total_c.astype(jnp.bfloat16))

    def to_gm(start, step, value):
        gm_all[z, start : start + step, :] = value

    conv(go_t, 0, True, to_gm)
    for i in range(1, heads):
        spread(gm_all, gm_s, gm_r, i).start()

    def penalty(query_block, key_block):
        inside = (query_block >= 0) & (query_block < frames) & (key_block >= 0) & (key_block < frames)
        safe = lax.rem(query_block + frames, frames)
        number = cnt_ref[0, safe]
        hit = False
        for entry in range(pat_ref.shape[2]):
            hit = hit | ((pat_ref[0, safe, entry] == key_block) & (entry < number))
        return jnp.where(inside & hit, 0.0, HUGE)

    for n, o in enumerate(ORDER):
        slot = REACH + o
        if o != 0:
            shift(kv, kv_s, kv_r, -o).wait_recv()
        pen = penalty(f, f + o)

        def forward(i, carry, slot=slot, first=n == 0, pen=pen):
            at = pl.ds(pl.multiple_of(i * R, R), R)
            s = dot(qm[at, :], kv[slot, 0], NT)
            m = jnp.max(s, axis=1, keepdims=True) - pen
            if not first:
                old = peak[at, :]
                m = jnp.maximum(old, m)
            p = jnp.exp(s - (m + pen))
            l = jnp.sum(p, axis=1, keepdims=True)
            pb = p.astype(jnp.bfloat16)
            probs[slot, at, :] = pb
            pv = dot(pb, kv[slot, 1], NN)
            if not first:
                fade = jnp.exp(old - m)
                l = l + total[at, :] * fade
                pv = pv + acc[at, :] * fade
            peak[at, :] = m
            peaks[slot, at, :] = m
            total[at, :] = l
            acc[at, :] = pv
            return carry

        lax.fori_loop(0, 2 * rows // R, forward, 0)

    inv0 = 1.0 / total[0:rows, :]
    inv1 = 1.0 / total[rows : 2 * rows, :]
    att = jnp.where(low, acc[0:rows, :] * inv0, acc[rows : 2 * rows, :] * inv1).astype(jnp.bfloat16)
    at_all[z] = att
    for i in range(1, heads):
        spread(at_all, at_s, at_r, i).start()

    for i in range(1, heads):
        spread_arrived(gm_all, gm_s, gm_r, i).wait_recv()
    grad = jnp.zeros((rows, width), jnp.float32)
    for i in range(heads):
        grad = grad + dot(gm_all[i], w_ref[:, i * width : (i + 1) * width], NT)
    grad_bf = grad.astype(jnp.bfloat16)
    do[REACH] = grad_bf
    for o in NEIGHBOURS:
        shift(do, do_s, do_r, o).start()
    split_heads(grad_bf, dom)

    product = grad_bf.astype(jnp.float32) * att.astype(jnp.float32)
    delta[0:rows, :] = jnp.sum(jnp.where(low, product, 0.0), axis=1, keepdims=True)
    delta[rows : 2 * rows, :] = jnp.sum(jnp.where(low, 0.0, product), axis=1, keepdims=True)
    logsum = peak[...] + jnp.log(total[...])
    logs = jnp.where(low, logsum[0:rows, :], logsum[rows : 2 * rows, :]).T
    prod_t = product.T
    stats[REACH, 0:1, :] = logs[0:1, :]
    stats[REACH, 1:2, :] = logs[HEAD_DIM : HEAD_DIM + 1, :]
    stats[REACH, 2:3, :] = jnp.sum(prod_t[0:HEAD_DIM, :], axis=0, keepdims=True)
    stats[REACH, 3:4, :] = jnp.sum(prod_t[HEAD_DIM:, :], axis=0, keepdims=True)
    stats[REACH, 4:8, :] = jnp.zeros((4, rows), jnp.float32)
    for o in NEIGHBOURS:
        shift(stats, st_s, st_r, o).start()

    def back_queries(i, carry):
        at = pl.ds(pl.multiple_of(i * R, R), R)
        out = jnp.zeros((R, width), jnp.float32)
        factor = HEAD_DIM**-0.5 / total[at, :]
        for slot in range(SPAN):
            dp = dot(dom[at, :], kv[slot, 1], NT)
            ds = (probs[slot, at, :].astype(jnp.float32) * (dp - delta[at, :])).astype(jnp.bfloat16)
            scale = factor * jnp.exp(peaks[slot, at, :] - peak[at, :])
            out = out + scale * dot(ds, kv[slot, 0], NN)
        acc[at, :] = out
        return carry

    lax.fori_loop(0, 2 * rows // R, back_queries, 0)
    dq_ref[...] = jnp.where(low, acc[0:rows, :], acc[rows : 2 * rows, :]).astype(jnp.bfloat16)

    for i in range(1, heads):
        src = zrel(i)
        remote(w_ref.at[:, own_cols], wcol.at[src], w_s.at[i], w_r.at[src], (f, src)).wait_recv()
    for i in range(1, heads):
        spread_arrived(at_all, at_s, at_r, i).wait_recv()
    mix = jnp.zeros((rows, width), jnp.float32)
    for i in range(heads):
        mix = mix + dot(at_all[i], wcol[i], NN)
    mixed[...] = mix.astype(jnp.bfloat16)
    for o in (1, -1):
        edge(mixed, 1, o).start()

    for n, o in enumerate(ORDER):
        slot = REACH + o
        if o != 0:
            shift(qs, q_s, q_r, -o).wait_recv()
            shift(do, do_s, do_r, -o).wait_recv()
            shift(stats, st_s, st_r, -o).wait_recv()
        pen = penalty(f + o, f)
        for h in range(2):

            def back_keys(i, carry, slot=slot, first=n == 0, pen=pen, h=h):
                at = pl.ds(pl.multiple_of(h * rows + i * R, R), R)
                st = dot(km[at, :], qs[slot], NT)
                pt = jnp.exp(st - (stats[slot, h : h + 1, :] + pen))
                dpt = dot(vm[at, :], do[slot], NT)
                dst = (pt * (dpt - stats[slot, 2 + h : 3 + h, :])).astype(jnp.bfloat16)
                gv = dot(pt.astype(jnp.bfloat16), do[slot], NN)
                gk = dot(dst, qs[slot], NN)
                if not first:
                    gv = gv + acc[at, :]
                    gk = gk + acc2[at, :]
                acc[at, :] = gv
                acc2[at, :] = gk
                return carry

            lax.fori_loop(0, rows // R, back_keys, 0)
    dv_ref[...] = jnp.where(low, acc[0:rows, :], acc[rows : 2 * rows, :]).astype(jnp.bfloat16)
    dk_ref[...] = jnp.where(low, acc2[0:rows, :], acc2[rows : 2 * rows, :]).astype(jnp.bfloat16)

    def to_mixed(start, step, value):
        mixed_out[start : start + step, :] = value

    mixed_out = go_t
    for o in (1, -1):
        edge(go_t, 0, o).wait_send()
    conv(mixed, 1, False, to_mixed)
    co_ref[...] = go_t[...].T

    for o in (1, -1):
        edge(mixed, 1, o).wait_send()
    for o in NEIGHBOURS:
        shift(kv, kv_s, kv_r, o).wait_send()
        shift(qs, q_s, q_r, o).wait_send()
        shift(do, do_s, do_r, o).wait_send()
        shift(stats, st_s, st_r, o).wait_send()
    for i in range(1, heads):
        weight(i).wait_send()
        spread(gm_all, gm_s, gm_r, i).wait_send()
        spread(at_all, at_s, at_r, i).wait_send()


def on_device(queries, keys, values, out_weight, conv_kernel, grad_out, pattern, counts):
    _, rows, width = queries.shape
    frames, heads = lax.axis_size("frame"), lax.axis_size("head")
    bf, f32 = jnp.bfloat16, jnp.float32
    block = (rows, width)
    vmem = pl.BlockSpec(memory_space=pltpu.VMEM)
    smem = pl.BlockSpec(memory_space=pltpu.SMEM)
    dma = pltpu.SemaphoreType.DMA
    conv_out, dq, dk, dv = pl.pallas_call(
        partial(kernel, frames, heads),
        out_shape=[
            jax.ShapeDtypeStruct((width, rows), bf),
            jax.ShapeDtypeStruct(block, bf),
            jax.ShapeDtypeStruct(block, bf),
            jax.ShapeDtypeStruct(block, bf),
        ],
        in_specs=[vmem] * 6 + [smem] * 2,
        out_specs=[vmem] * 4,
        scratch_shapes=[
            pltpu.VMEM((SPAN, 2) + block, bf),
            pltpu.VMEM((SPAN,) + block, bf),
            pltpu.VMEM((SPAN,) + block, bf),
            pltpu.VMEM((SPAN, 8, rows), f32),
            pltpu.VMEM((heads,) + block, bf),
            pltpu.VMEM((heads,) + block, bf),
            pltpu.VMEM((heads, width, width), bf),
            pltpu.VMEM(block, bf),
            pltpu.VMEM(block, bf),
            pltpu.VMEM((2, 2, RIM, width), bf),
            pltpu.VMEM((rows + 2 * RIM, width), f32),
            pltpu.VMEM((32, width), f32),
            pltpu.VMEM((2 * rows, width), bf),
            pltpu.VMEM((2 * rows, width), bf),
            pltpu.VMEM((2 * rows, width), bf),
            pltpu.VMEM((2 * rows, width), bf),
            pltpu.VMEM((SPAN, 2 * rows, rows), bf),
            pltpu.VMEM((SPAN, 2 * rows, 1), f32),
            pltpu.VMEM((2 * rows, 1), f32),
            pltpu.VMEM((2 * rows, 1), f32),
            pltpu.VMEM((2 * rows, width), f32),
            pltpu.VMEM((2 * rows, 1), f32),
            pltpu.VMEM((2 * rows, width), f32),
            dma((SPAN,)),
            dma((SPAN,)),
            dma((SPAN,)),
            dma((SPAN,)),
            dma((SPAN,)),
            dma((SPAN,)),
            dma((SPAN,)),
            dma((SPAN,)),
            dma((heads,)),
            dma((heads,)),
            dma((heads,)),
            dma((heads,)),
            dma((heads,)),
            dma((heads,)),
            dma((2, 2)),
            dma((2, 2)),
        ],
        compiler_params=pltpu.CompilerParams(
            collective_id=0, has_side_effects=True, vmem_limit_bytes=48 * 1024 * 1024
        ),
    )(
        queries.reshape(block),
        keys.reshape(block),
        values.reshape(block),
        out_weight,
        conv_kernel,
        grad_out.reshape(width, rows),
        pattern,
        counts,
    )
    return (
        conv_out.reshape(grad_out.shape),
        dq.reshape(queries.shape),
        dk.reshape(keys.shape),
        dv.reshape(values.shape),
    )


def solution(mesh):
    return jax.shard_map(
        on_device,
        mesh=mesh,
        in_specs=(
            P(None, "frame", "head"),
            P(None, "frame", "head"),
            P(None, "frame", "head"),
            P("head", None),
            P(None, "head"),
            P("head", None, "frame"),
            P(),
            P(),
        ),
        out_specs=(
            P("head", None, "frame"),
            P(None, "frame", "head"),
            P(None, "frame", "head"),
            P(None, "frame", "head"),
        ),
        check_vma=False,
    )
```

time: 240 us -> 90.1 us (0.38)
  the two profiles are of different devices: /device:TPU:21 before, /device:TPU:1 now
where the time goes in v1:
time: 90.1 us; the launch traced here: 89.8 us
  Pallas kernels  80.6 us (89%)
  local copies, waits for them, and re-layouts  8.56 us (10%)
    pallas_call x1, Pallas kernels, on_device(): pl.pallas_call(partial(kernel, frames, heads), out_shape=[jax.ShapeDtypeS...  80.6 us
    unnamed x21, local copies, waits for them, and re-layouts  8.56 us

profile of v1, /device:TPU:1, one launch (start us, length us, event | category | flops | bytes accessed | tf_op | source)
XLA Modules:
  0.0 89.8 jit_solution(18010942480815704597)
XLA Ops:
  0.6 0.0 copy-start.7
  0.6 0.7 copy-done.7
  1.3 0.0 copy-start.5
  1.3 0.0 copy-start.6
  1.3 0.1 copy.12.pat_ref
  1.4 0.6 copy-done.5
  2.0 0.0 copy-done.6
  2.0 0.0 copy-start
  2.0 0.9 %copy-done = bf16[128,1024]{1,0:T(8,128)(2,1)S(1)} copy-done((bf16[128,1024]{1,0:T(8,128)(2,1)S(1)}, bf16[128,1024]{1,0:T(8,128)(2,1)}, u32[]{:S(2)}) %copy-start) | copy-done | bytes 262168
  3.0 0.0 copy-start.1
  3.0 0.9 %copy-done.1 = bf16[1,512,128]{2,1,0:T(8,128)(2,1)S(1)} copy-done((bf16[1,512,128]{2,1,0:T(8,128)(2,1)S(1)}, bf16[1,512,128]{2,1,0:T(8,128)(2,1)}, u32[]{:S(2)}) %copy-start.1) | copy-done | bytes 131096
  3.9 0.0 copy-start.2
  3.9 0.9 %copy-done.2 = bf16[1,512,128]{2,1,0:T(8,128)(2,1)S(1)} copy-done((bf16[1,512,128]{2,1,0:T(8,128)(2,1)S(1)}, bf16[1,512,128]{2,1,0:T(8,128)(2,1)}, u32[]{:S(2)}) %copy-start.2) | copy-done | bytes 131096
  4.8 0.0 copy-start.3
  4.8 0.9 %copy-done.3 = bf16[1,512,128]{2,1,0:T(8,128)(2,1)S(1)} copy-done((bf16[1,512,128]{2,1,0:T(8,128)(2,1)S(1)}, bf16[1,512,128]{2,1,0:T(8,128)(2,1)}, u32[]{:S(2)}) %copy-start.3) | copy-done | bytes 131096
  5.7 0.0 copy-start.4
  5.7 0.9 %copy-done.4 = bf16[128,1,512]{2,0,1:T(8,128)(2,1)S(1)} copy-done((bf16[128,1,512]{2,0,1:T(8,128)(2,1)S(1)}, bf16[128,1,512]{2,0,1:T(8,128)(2,1)}, u32[]{:S(2)}) %copy-start.4) | copy-done | bytes 131096
  6.6 80.6 %shard_map.111 = (bf16[128,512]{1,0:T(8,128)(2,1)S(1)}, bf16[512,128]{1,0:T(8,128)(2,1)S(1)}, bf16[512,128]{1,0:T(8,128)(2,1)S(1)}, bf16[512,128]{1,0:T(8,128)(2,1)S(1)}) custom-call(bf16[512,128]{1,0:T(8,128)(2,1)S(1)} %bitcast.12, bf16[512,128]{1,0:T(8,128)(2,1)S(1)} %bitcast.13, bf16[512,128]{1,0:T(8,128)(2,1)S(1)} %bitcast.14, ...), custom_call_target="tpu_custom_call" | custom-call | tf_op jit(solution)/shard_map/pallas_call | solution.py:336
  87.2 0.7 copy.17
  87.9 0.7 copy.18
  88.5 0.7 copy.19
  89.2 0.7 copy.20
Async XLA Ops:
  0.6 0.7 copy-start.7
  1.3 0.7 copy-start.5
  1.3 0.7 copy-start.6
  2.0 1.0 %copy-start = (bf16[128,1024]{1,0:T(8,128)(2,1)S(1)}, bf16[128,1024]{1,0:T(8,128)(2,1)}, u32[]{:S(2)}) copy-start(bf16[128,1024]{1,0:T(8,128)(2,1)} %w_ref.1) | copy-start | bytes 786436
  3.0 0.9 %copy-start.1 = (bf16[1,512,128]{2,1,0:T(8,128)(2,1)S(1)}, bf16[1,512,128]{2,1,0:T(8,128)(2,1)}, u32[]{:S(2)}) copy-start(bf16[1,512,128]{2,1,0:T(8,128)(2,1)} %param.8) | copy-start | bytes 393220
  3.9 0.9 %copy-start.2 = (bf16[1,512,128]{2,1,0:T(8,128)(2,1)S(1)}, bf16[1,512,128]{2,1,0:T(8,128)(2,1)}, u32[]{:S(2)}) copy-start(bf16[1,512,128]{2,1,0:T(8,128)(2,1)} %param.9) | copy-start | bytes 393220
  4.8 0.9 %copy-start.3 = (bf16[1,512,128]{2,1,0:T(8,128)(2,1)S(1)}, bf16[1,512,128]{2,1,0:T(8,128)(2,1)}, u32[]{:S(2)}) copy-start(bf16[1,512,128]{2,1,0:T(8,128)(2,1)} %param.10) | copy-start | bytes 393220
  5.7 0.9 %copy-start.4 = (bf16[128,1,512]{2,0,1:T(8,128)(2,1)S(1)}, bf16[128,1,512]{2,0,1:T(8,128)(2,1)}, u32[]{:S(2)}) copy-start(bf16[128,1,512]{2,0,1:T(8,128)(2,1)} %param.13) | copy-start | bytes 393220

commit v2 on v1

v2 whole, which is shorter than its diff:
```python
from functools import partial, reduce

import jax
import jax.numpy as jnp
from jax import lax
from jax.experimental import pallas as pl
from jax.experimental.pallas import tpu as pltpu
from jax.sharding import PartitionSpec as P

HEAD_DIM = 64
KERNEL = 31
SPAN = 7
HUGE = 1e30
MESH = pl.DeviceIdType.MESH
RIM = 16
HOPS = 4

NT = (((1,), (1,)), ((), ()))
NN = (((1,), (0,)), ((), ()))

OWN, PAIR, UP, DOWN, PAIR_UP, PAIR_DOWN, FAR = range(SPAN)
GROUPS = ((OWN,), (PAIR,), (UP, DOWN), (PAIR_UP, PAIR_DOWN), (FAR,))


def dot(a, b, dims):
    return lax.dot_general(a, b, dims, preferred_element_type=jnp.float32)


def remote(src, dst, s, r, dev):
    return pltpu.make_async_remote_copy(
        src_ref=src, dst_ref=dst, send_sem=s, recv_sem=r, device_id=dev, device_id_type=MESH
    )


def kernel(
    frames,
    heads,
    q_hbm,
    k_hbm,
    v_hbm,
    w_hbm,
    t_hbm,
    g_hbm,
    pat_ref,
    cnt_ref,
    co_hbm,
    dq_hbm,
    dk_hbm,
    dv_hbm,
    w_ref,
    t_ref,
    g_ref,
    co_ref,
    dq_ref,
    dk_ref,
    dv_ref,
    kv,
    kt,
    vt,
    qs,
    do,
    stats,
    gm_all,
    at_all,
    wcol,
    wcol_t,
    go_t,
    mixed,
    conv_tmp,
    halo,
    pad,
    taps,
    qmt,
    dmt,
    km,
    vm,
    probs,
    peaks,
    peak,
    total,
    acc,
    gk_acc,
    gv_acc,
    in_s,
    out_s,
    kv_s,
    kv_r,
    q_s,
    q_r,
    do_s,
    do_r,
    st_s,
    st_r,
    w_s,
    w_r,
    gm_s,
    gm_r,
    at_s,
    at_r,
    h_s,
    h_r,
):
    f = lax.axis_index("frame")
    z = lax.axis_index("head")
    rows, width = kv.shape[2], kv.shape[3]
    odd = lax.rem(f, 2)
    sign = 2 * odd - 1

    def fdev(o):
        return (lax.rem(f + o + frames, frames), z)

    def zrel(i):
        return lax.rem(z + i + heads, heads)

    def part(index, size=width, start=0):
        return pl.ds(pl.multiple_of(index * width + start, size), size)

    offsets = (0, -sign, 2, -2, 2 - sign, -2 - sign, 3 * sign)

    loads = [
        pltpu.make_async_copy(src, dst, in_s.at[n])
        for n, (src, dst) in enumerate(
            (
                (g_hbm, g_ref),
                (k_hbm, kv.at[OWN, 0]),
                (v_hbm, kv.at[OWN, 1]),
                (q_hbm, qs.at[OWN]),
                (t_hbm, t_ref),
                (w_hbm, w_ref),
            )
        )
    ]
    for load in loads:
        load.start()

    barrier = pltpu.get_barrier_semaphore()
    for o in offsets[1:]:
        pl.semaphore_signal(barrier, inc=1, device_id=fdev(o), device_id_type=MESH)
    for i in range(1, heads):
        pl.semaphore_signal(barrier, inc=1, device_id=(f, zrel(i)), device_id_type=MESH)

    def route(buf, s, r, role):
        src, o = {
            PAIR: (OWN, -sign),
            DOWN: (OWN, 2),
            UP: (OWN, -2),
            PAIR_UP: (UP, -sign),
            PAIR_DOWN: (DOWN, -sign),
            FAR: (UP + odd, sign),
        }[role]
        return remote(buf.at[src], buf.at[role], s.at[role], r.at[role], fdev(o))

    FIRST, SECOND = (UP, DOWN, PAIR), (FAR, PAIR_UP, PAIR_DOWN)

    def direct(role):
        o = {
            PAIR: -sign,
            DOWN: 2,
            UP: -2,
            PAIR_DOWN: 2 - sign,
            PAIR_UP: -2 - sign,
            FAR: 3 * sign,
        }[role]
        return remote(stats.at[OWN], stats.at[role], st_s.at[role], st_r.at[role], fdev(o))

    def edge(buf, which, o):
        src = buf.at[pl.ds(rows - RIM, RIM)] if o == 1 else buf.at[pl.ds(0, RIM)]
        side = 0 if o == 1 else 1
        return remote(src, halo.at[which, side], h_s.at[which, side], h_r.at[which, side], fdev(o))

    def weight(i):
        there = zrel(i)
        return remote(w_ref.at[:, part(there)], wcol.at[z], w_s.at[i], w_r.at[z], (f, there))

    def hop(buf, s, r, way, k, arrived=False):
        back = k if arrived else k - 1
        origin = zrel(-back if way == 0 else back)
        half = width // 2
        at = part(origin) if k < HOPS else part(origin, half, half * way)
        return remote(
            buf.at[at], buf.at[at], s.at[way, k - 1], r.at[way, k - 1], (f, zrel(1 if way == 0 else -1))
        )

    def pass_on(buf, s, r, k):
        for way in range(2):
            if k > 1:
                hop(buf, s, r, way, k - 1, True).wait_recv()
            hop(buf, s, r, way, k).start()

    def penalty(query_block, key_block):
        inside = (query_block >= 0) & (query_block < frames) & (key_block >= 0) & (key_block < frames)
        safe = lax.rem(query_block + frames, frames)
        number = cnt_ref[0, safe]
        hit = False
        for entry in range(pat_ref.shape[2]):
            hit = hit | ((pat_ref[0, safe, entry] == key_block) & (entry < number))
        return jnp.where(inside & hit, 0.0, HUGE)

    def conv(src, which, flip, out):
        pad[RIM : RIM + rows, :] = src[...].astype(jnp.float32)
        for o in (1, -1):
            edge(src, which, o).wait_recv()
        left = halo[which, 0].astype(jnp.float32)
        right = halo[which, 1].astype(jnp.float32)
        pad[0:RIM, :] = jnp.where(f > 0, left, 0.0)
        pad[RIM + rows : 2 * RIM + rows, :] = jnp.where(f < frames - 1, right, 0.0)
        step = 64
        for c in range(rows // step):
            total_c = jnp.zeros((step, width), jnp.float32)
            for t in range(KERNEL):
                tap = KERNEL - 1 - t if flip else t
                total_c = total_c + taps[tap : tap + 1, :] * pad[c * step + t + 1 : c * step + t + 1 + step, :]
            out[c * step : c * step + step, :] = total_c.astype(jnp.bfloat16)

    def head_columns(x, dst):
        dst[0:HEAD_DIM, 0:rows] = x[0:HEAD_DIM, :]
        dst[HEAD_DIM:width, rows : 2 * rows] = x[HEAD_DIM:width, :]
        dst[0:HEAD_DIM, rows : 2 * rows] = jnp.zeros((HEAD_DIM, rows), jnp.bfloat16)
        dst[HEAD_DIM:width, 0:rows] = jnp.zeros((HEAD_DIM, rows), jnp.bfloat16)

    low = lax.broadcasted_iota(jnp.int32, (rows, width), 1) < HEAD_DIM

    def head_rows(x, dst):
        x = x.astype(jnp.float32)
        dst[0:rows, :] = jnp.where(low, x, 0.0).astype(jnp.bfloat16)
        dst[rows : 2 * rows, :] = jnp.where(low, 0.0, x).astype(jnp.bfloat16)

    def by_head(row):
        return jnp.concatenate(
            [
                jnp.broadcast_to(row[:, 0:rows], (HEAD_DIM, rows)),
                jnp.broadcast_to(row[:, rows : 2 * rows], (HEAD_DIM, rows)),
            ],
            axis=0,
        )

    def forward(group):
        roles = GROUPS[group]
        for role in roles:
            vt[role] = kv[role, 1].T
        scores = [dot(kv[role, 0], qmt[...], NN) for role in roles]
        pens = [penalty(f, f + offsets[role]) for role in roles]
        m = reduce(
            jnp.maximum, [jnp.max(s, axis=0, keepdims=True) - pen for s, pen in zip(scores, pens)]
        )
        if group > 0:
            old = peak[...]
            m = jnp.maximum(old, m)
        sums, outs = [], []
        for role, s, pen in zip(roles, scores, pens):
            p = jnp.exp(s - (m + pen))
            sums.append(jnp.sum(p, axis=0, keepdims=True))
            weights = p.astype(jnp.bfloat16)
            probs[role] = weights
            outs.append(
                jnp.concatenate(
                    [
                        dot(vt[role, 0:HEAD_DIM, :], weights[:, 0:rows], NN),
                        dot(vt[role, HEAD_DIM:width, :], weights[:, rows : 2 * rows], NN),
                    ],
                    axis=0,
                )
            )
        row_sum, out = reduce(jnp.add, sums), reduce(jnp.add, outs)
        if group > 0:
            fade = jnp.exp(old - m)
            row_sum = row_sum + total[...] * fade
            out = out + acc[...] * by_head(fade)
        peak[...] = m
        peaks[group] = m
        total[...] = row_sum
        acc[...] = out

    def back_queries(h):
        cols = slice(h * rows, h * rows + rows)
        feats = slice(h * HEAD_DIM, (h + 1) * HEAD_DIM)
        out = jnp.zeros((HEAD_DIM, rows), jnp.float32)
        factor = HEAD_DIM**-0.5 / total[:, cols]
        delta = stats[OWN, 2 + h : 3 + h, :]
        for group, roles in enumerate(GROUPS):
            scale = factor * jnp.exp(peaks[group, :, cols] - peak[:, cols])
            for role in roles:
                dp = dot(kv[role, 1], dmt[:, cols], NN)
                ds = (probs[role, :, cols].astype(jnp.float32) * (dp - delta)).astype(jnp.bfloat16)
                out = out + scale * dot(kt[role, feats, :], ds, NN)
        acc[feats, :] = out

    def back_keys(role):
        pen = penalty(f + offsets[role], f)
        for h in range(2):
            at = slice(h * rows, h * rows + rows)
            st = dot(km[at, :], qs[role], NT)
            pt = jnp.exp(st - (stats[role, h : h + 1, :] + pen))
            dpt = dot(vm[at, :], do[role], NT)
            dst = (pt * (dpt - stats[role, 2 + h : 3 + h, :])).astype(jnp.bfloat16)
            gv = dot(pt.astype(jnp.bfloat16), do[role], NN)
            gk = dot(dst, qs[role], NN)
            if role != OWN:
                gv = gv + gv_acc[at, :]
                gk = gk + gk_acc[at, :]
            gv_acc[at, :] = gv
            gk_acc[at, :] = gk

    loads[0].wait()
    go_t[...] = g_ref[...].T
    loads[1].wait()
    loads[2].wait()
    pl.semaphore_wait(barrier, SPAN - 1 + heads - 1)
    for o in (1, -1):
        edge(go_t, 0, o).start()
    for role in FIRST:
        route(kv, kv_s, kv_r, role).start()
    loads[5].wait()
    for i in range(1, heads):
        weight(i).start()
    loads[3].wait()
    loads[4].wait()
    taps[0:KERNEL, :] = t_ref[...].astype(jnp.float32)
    qs[OWN] = (qs[OWN].astype(jnp.float32) * HEAD_DIM**-0.5).astype(jnp.bfloat16)
    head_columns(qs[OWN].T, qmt)

    conv(go_t, 0, True, conv_tmp)
    gm_all[part(z), :] = conv_tmp[...].T
    pass_on(gm_all, gm_s, gm_r, 1)

    forward(0)
    route(kv, kv_s, kv_r, PAIR).wait_recv()
    forward(1)
    route(kv, kv_s, kv_r, UP).wait_recv()
    route(kv, kv_s, kv_r, DOWN).wait_recv()
    for role in SECOND:
        route(kv, kv_s, kv_r, role).start()
    for role in FIRST:
        route(qs, q_s, q_r, role).start()
    forward(2)
    pass_on(gm_all, gm_s, gm_r, 2)
    route(kv, kv_s, kv_r, PAIR_UP).wait_recv()
    route(kv, kv_s, kv_r, PAIR_DOWN).wait_recv()
    forward(3)
    route(kv, kv_s, kv_r, FAR).wait_recv()
    forward(4)

    attended = (acc[...] * by_head(1.0 / total[...])).astype(jnp.bfloat16)
    at_all[part(z), :] = attended
    pass_on(gm_all, gm_s, gm_r, 3)
    pass_on(at_all, at_s, at_r, 1)

    head_rows(kv[OWN, 0], km)
    head_rows(kv[OWN, 1], vm)
    for role in range(SPAN):
        kt[role] = kv[role, 0].T
    logsum = peak[...] + jnp.log(total[...])
    stats[OWN, 0:1, :] = logsum[:, 0:rows]
    stats[OWN, 1:2, :] = logsum[:, rows : 2 * rows]
    stats[OWN, 4:8, :] = jnp.zeros((4, rows), jnp.float32)
    wcol[z] = w_ref[:, part(z)]
    route(qs, q_s, q_r, UP).wait_recv()
    route(qs, q_s, q_r, DOWN).wait_recv()
    for role in SECOND:
        route(qs, q_s, q_r, role).start()
    pass_on(gm_all, gm_s, gm_r, 4)
    for i in range(1, heads):
        src = zrel(i)
        remote(w_ref.at[:, part(z)], wcol.at[src], w_s.at[i], w_r.at[src], (f, src)).wait_recv()
    for i in range(heads):
        wcol_t[:, i * width : (i + 1) * width] = wcol[i].T
    for way in range(2):
        hop(gm_all, gm_s, gm_r, way, HOPS, True).wait_recv()

    grad_t = dot(w_ref[...], gm_all[...], NN).astype(jnp.bfloat16)
    do[OWN] = grad_t.T
    for role in FIRST:
        route(do, do_s, do_r, role).start()
    product = grad_t.astype(jnp.float32) * attended.astype(jnp.float32)
    stats[OWN, 2:3, :] = jnp.sum(product[0:HEAD_DIM, :], axis=0, keepdims=True)
    stats[OWN, 3:4, :] = jnp.sum(product[HEAD_DIM:width, :], axis=0, keepdims=True)
    for role in range(1, SPAN):
        direct(role).start()
    head_columns(grad_t, dmt)

    pass_on(at_all, at_s, at_r, 2)
    back_queries(0)
    pass_on(at_all, at_s, at_r, 3)
    route(do, do_s, do_r, UP).wait_recv()
    route(do, do_s, do_r, DOWN).wait_recv()
    for role in SECOND:
        route(do, do_s, do_r, role).start()
    back_queries(1)
    dq_ref[...] = acc[...].T.astype(jnp.bfloat16)
    stores = [
        pltpu.make_async_copy(src, dst, out_s.at[n])
        for n, (src, dst) in enumerate(
            ((dq_ref, dq_hbm), (dk_ref, dk_hbm), (dv_ref, dv_hbm), (co_ref, co_hbm))
        )
    ]
    stores[0].start()
    pass_on(at_all, at_s, at_r, 4)
    back_keys(OWN)

    def keys_of(role):
        if role in (PAIR, PAIR_UP, PAIR_DOWN, FAR):
            route(qs, q_s, q_r, role).wait_recv()
            route(do, do_s, do_r, role).wait_recv()
        direct(role).wait_recv()
        back_keys(role)

    keys_of(PAIR)
    keys_of(UP)
    keys_of(DOWN)

    for way in range(2):
        hop(at_all, at_s, at_r, way, HOPS, True).wait_recv()
    mixed[...] = dot(wcol_t[...], at_all[...], NN).T.astype(jnp.bfloat16)
    for o in (1, -1):
        edge(mixed, 1, o).start()

    keys_of(PAIR_UP)
    keys_of(PAIR_DOWN)
    keys_of(FAR)
    dv_ref[...] = jnp.where(low, gv_acc[0:rows, :], gv_acc[rows : 2 * rows, :]).astype(jnp.bfloat16)
    dk_ref[...] = jnp.where(low, gk_acc[0:rows, :], gk_acc[rows : 2 * rows, :]).astype(jnp.bfloat16)
    stores[1].start()
    stores[2].start()

    conv(mixed, 1, False, conv_tmp)
    co_ref[...] = conv_tmp[...].T
    stores[3].start()

    for o in (1, -1):
        edge(go_t, 0, o).wait_send()
        edge(mixed, 1, o).wait_send()
    for role in range(1, SPAN):
        route(kv, kv_s, kv_r, role).wait_send()
        route(qs, q_s, q_r, role).wait_send()
        route(do, do_s, do_r, role).wait_send()
        direct(role).wait_send()
    for i in range(1, heads):
        weight(i).wait_send()
    for k in range(1, HOPS + 1):
        for way in range(2):
            hop(gm_all, gm_s, gm_r, way, k).wait_send()
            hop(at_all, at_s, at_r, way, k).wait_send()
    for store in stores:
        store.wait()


def on_device(queries, keys, values, out_weight, conv_kernel, grad_out, pattern, counts):
    _, rows, width = queries.shape
    frames, heads = lax.axis_size("frame"), lax.axis_size("head")
    bf, f32 = jnp.bfloat16, jnp.float32
    block, tall = (rows, width), (width, rows)
    hbm = pl.BlockSpec(memory_space=pltpu.HBM)
    smem = pl.BlockSpec(memory_space=pltpu.SMEM)
    dma = pltpu.SemaphoreType.DMA
    conv_out, dq, dk, dv = pl.pallas_call(
        partial(kernel, frames, heads),
        out_shape=[
            jax.ShapeDtypeStruct(tall, bf),
            jax.ShapeDtypeStruct(block, bf),
            jax.ShapeDtypeStruct(block, bf),
            jax.ShapeDtypeStruct(block, bf),
        ],
        in_specs=[hbm] * 6 + [smem] * 2,
        out_specs=[hbm] * 4,
        scratch_shapes=[
            pltpu.VMEM(out_weight.shape, bf),
            pltpu.VMEM(conv_kernel.shape, bf),
            pltpu.VMEM(tall, bf),
            pltpu.VMEM(tall, bf),
            pltpu.VMEM(block, bf),
            pltpu.VMEM(block, bf),
            pltpu.VMEM(block, bf),
            pltpu.VMEM((SPAN, 2) + block, bf),
            pltpu.VMEM((SPAN,) + tall, bf),
            pltpu.VMEM((SPAN,) + tall, bf),
            pltpu.VMEM((SPAN,) + block, bf),
            pltpu.VMEM((SPAN,) + block, bf),
            pltpu.VMEM((SPAN, 8, rows), f32),
            pltpu.VMEM((heads * width, rows), bf),
            pltpu.VMEM((heads * width, rows), bf),
            pltpu.VMEM((heads, width, width), bf),
            pltpu.VMEM((width, heads * width), bf),
            pltpu.VMEM(block, bf),
            pltpu.VMEM(block, bf),
            pltpu.VMEM(block, bf),
            pltpu.VMEM((2, 2, RIM, width), bf),
            pltpu.VMEM((rows + 2 * RIM, width), f32),
            pltpu.VMEM((32, width), f32),
            pltpu.VMEM((width, 2 * rows), bf),
            pltpu.VMEM((width, 2 * rows), bf),
            pltpu.VMEM((2 * rows, width), bf),
            pltpu.VMEM((2 * rows, width), bf),
            pltpu.VMEM((SPAN, rows, 2 * rows), bf),
            pltpu.VMEM((len(GROUPS), 1, 2 * rows), f32),
            pltpu.VMEM((1, 2 * rows), f32),
            pltpu.VMEM((1, 2 * rows), f32),
            pltpu.VMEM(tall, f32),
            pltpu.VMEM((2 * rows, width), f32),
            pltpu.VMEM((2 * rows, width), f32),
            dma((6,)),
            dma((4,)),
        ]
        + [dma((SPAN,))] * 8
        + [dma((heads,))] * 2
        + [dma((2, HOPS))] * 4
        + [dma((2, 2))] * 2,
        compiler_params=pltpu.CompilerParams(
            collective_id=0, has_side_effects=True, vmem_limit_bytes=56 * 1024 * 1024
        ),
    )(
        queries.reshape(block),
        keys.reshape(block),
        values.reshape(block),
        out_weight,
        conv_kernel,
        grad_out.reshape(width, rows),
        pattern,
        counts,
    )
    return (
        conv_out.reshape(grad_out.shape),
        dq.reshape(queries.shape),
        dk.reshape(keys.shape),
        dv.reshape(values.shape),
    )


def solution(mesh):
    return jax.shard_map(
        on_device,
        mesh=mesh,
        in_specs=(
            P(None, "frame", "head"),
            P(None, "frame", "head"),
            P(None, "frame", "head"),
            P("head", None),
            P(None, "head"),
            P("head", None, "frame"),
            P(),
            P(),
        ),
        out_specs=(
            P("head", None, "frame"),
            P(None, "frame", "head"),
            P(None, "frame", "head"),
            P(None, "frame", "head"),
        ),
        check_vma=False,
    )
```

time: 90.1 us -> 63.7 us (0.71)
  Pallas kernels: 80.6 us -> 56.9 us
  local copies, waits for them, and re-layouts: 8.56 us -> 5.53 us
    pallas_call x1, Pallas kernels: 80.6 us -> 56.9 us  [on_device(): pl.pallas_call(partial(kernel, frames, heads), out_shape=[jax.ShapeDtypeS...]
    unnamed x21 -> x13, local copies, waits for them, and re-layouts: 8.56 us -> 5.53 us
where the time goes in v2:
time: 63.7 us; the launch traced here: 63.1 us
  Pallas kernels  56.9 us (89%)
  local copies, waits for them, and re-layouts  5.53 us (9%)
  between operations  0.66 us (1%)
    pallas_call x1, Pallas kernels, on_device(): pl.pallas_call(partial(kernel, frames, heads), out_shape=[jax.ShapeDtypeS...  56.9 us
    unnamed x13, local copies, waits for them, and re-layouts  5.53 us

profile of v2, /device:TPU:1, one launch (start us, length us, event | category | flops | bytes accessed | tf_op | source)
XLA Modules:
  0.0 63.1 jit_solution(3229271903922931383)
XLA Ops:
  0.6 0.0 copy-start.3
  0.6 0.7 %copy-done.3 = s32[1,32,7]{1,0,2:T(1,128)S(1)} copy-done((s32[1,32,7]{1,0,2:T(1,128)S(1)}, s32[1,32,7]{1,0,2:T(1,128)}, u32[]{:S(2)}) %copy-start.3) | copy-done | bytes 920
  1.3 0.7 %copy.12.pat_ref = s32[1,32,7]{2,1,0:T(8,128)} copy(s32[1,32,7]{1,0,2:T(1,128)S(1)} %copy-done.3) | data formatting | bytes 1792 | tf_op args[6]
  2.0 56.9 %shard_map.111 = (bf16[128,512]{1,0:T(8,128)(2,1)}, bf16[512,128]{1,0:T(8,128)(2,1)}, bf16[512,128]{1,0:T(8,128)(2,1)}, bf16[512,128]{1,0:T(8,128)(2,1)}) custom-call(bf16[512,128]{1,0:T(8,128)(2,1)} %bitcast.12, bf16[512,128]{1,0:T(8,128)(2,1)} %bitcast.13, bf16[512,128]{1,0:T(8,128)(2,1)} %bitcast.14, bf16[128,1024]{1,0:T(8,128)(2,1)} %w_hbm.1, ...), custom_call_target="tpu_custom_call" | custom-call | tf_op jit(solution)/shard_map/pallas_call | solution.py:455
  58.9 0.0 copy-start.2
  58.9 1.6 %copy.17 = bf16[128,1,512]{2,0,1:T(8,128)(2,1)} copy(bf16[128,1,512]{2,0,1:T(8,128)(2,1)} %bitcast.11) | data formatting | bytes 262144
  60.5 0.0 copy-done.2
  60.5 0.0 copy-start.1
  60.5 0.7 %copy.18 = bf16[1,512,128]{2,1,0:T(8,128)(2,1)} copy(bf16[1,512,128]{2,1,0:T(8,128)(2,1)S(1)} %bitcast.10) | data formatting | bytes 262144
  61.2 0.3 copy-done.1
  61.5 0.0 copy-start
  61.5 0.7 %copy.19 = bf16[1,512,128]{2,1,0:T(8,128)(2,1)} copy(bf16[1,512,128]{2,1,0:T(8,128)(2,1)S(1)} %bitcast.9) | data formatting | bytes 262144
  62.1 0.3 copy-done
  62.4 0.7 %copy.20 = bf16[1,512,128]{2,1,0:T(8,128)(2,1)} copy(bf16[1,512,128]{2,1,0:T(8,128)(2,1)S(1)} %bitcast.8) | data formatting | bytes 262144
Async XLA Ops:
  0.6 0.7 %copy-start.3 = (s32[1,32,7]{1,0,2:T(1,128)S(1)}, s32[1,32,7]{1,0,2:T(1,128)}, u32[]{:S(2)}) copy-start(s32[1,32,7]{1,0,2:T(1,128)} %param.14) | copy-start | bytes 2692
  58.9 1.6 %copy-start.2 = (bf16[512,128]{1,0:T(8,128)(2,1)S(1)}, bf16[512,128]{1,0:T(8,128)(2,1)}, u32[]{:S(2)}) copy-start(bf16[512,128]{1,0:T(8,128)(2,1)} %get-tuple-element.9) | copy-start | bytes 393220
  60.5 1.0 %copy-start.1 = (bf16[512,128]{1,0:T(8,128)(2,1)S(1)}, bf16[512,128]{1,0:T(8,128)(2,1)}, u32[]{:S(2)}) copy-start(bf16[512,128]{1,0:T(8,128)(2,1)} %get-tuple-element.10) | copy-start | bytes 393220
  61.5 1.0 %copy-start = (bf16[512,128]{1,0:T(8,128)(2,1)S(1)}, bf16[512,128]{1,0:T(8,128)(2,1)}, u32[]{:S(2)}) copy-start(bf16[512,128]{1,0:T(8,128)(2,1)} %get-tuple-element.11) | copy-start | bytes 393220

commit v3 on v2

--- a/solution.py
+++ b/solution.py
@@ -13,7 +13,7 @@
 HUGE = 1e30
 MESH = pl.DeviceIdType.MESH
 RIM = 16
-HOPS = 4
+MAIL = 64
 
 NT = (((1,), (1,)), ((), ()))
 NN = (((1,), (0,)), ((), ()))
@@ -43,33 +43,32 @@
     g_hbm,
     pat_ref,
     cnt_ref,
-    co_hbm,
-    dq_hbm,
-    dk_hbm,
-    dv_hbm,
-    w_ref,
-    t_ref,
-    g_ref,
     co_ref,
     dq_ref,
     dk_ref,
     dv_ref,
+    w_ref,
+    t_ref,
+    g_ref,
     kv,
     kt,
     vt,
     qs,
     do,
     stats,
-    gm_all,
+    g_all,
     at_all,
+    mail,
+    mail_all,
+    ends,
+    rim,
+    rim_all,
     wcol,
     wcol_t,
-    go_t,
-    mixed,
     conv_tmp,
-    halo,
     pad,
     taps,
+    grad_acc,
     qmt,
     dmt,
     km,
@@ -82,7 +81,6 @@
     gk_acc,
     gv_acc,
     in_s,
-    out_s,
     kv_s,
     kv_r,
     q_s,
@@ -93,10 +91,14 @@
     st_r,
     w_s,
     w_r,
-    gm_s,
-    gm_r,
+    g_s,
+    g_r,
     at_s,
     at_r,
+    m_s,
+    m_r,
+    e_s,
+    e_r,
     h_s,
     h_r,
 ):
@@ -144,13 +146,13 @@
             PAIR: (OWN, -sign),
             DOWN: (OWN, 2),
             UP: (OWN, -2),
+            FAR: (OWN, 3 * sign),
             PAIR_UP: (UP, -sign),
             PAIR_DOWN: (DOWN, -sign),
-            FAR: (UP + odd, sign),
         }[role]
         return remote(buf.at[src], buf.at[role], s.at[role], r.at[role], fdev(o))
 
-    FIRST, SECOND = (UP, DOWN, PAIR), (FAR, PAIR_UP, PAIR_DOWN)
+    FIRST, SECOND = (UP, DOWN, PAIR, FAR), (PAIR_UP, PAIR_DOWN)
 
     def direct(role):
         o = {
@@ -163,47 +165,53 @@
         }[role]
         return remote(stats.at[OWN], stats.at[role], st_s.at[role], st_r.at[role], fdev(o))
 
-    def edge(buf, which, o):
-        src = buf.at[pl.ds(rows - RIM, RIM)] if o == 1 else buf.at[pl.ds(0, RIM)]
+    def edge(src, dst, which, o):
         side = 0 if o == 1 else 1
-        return remote(src, halo.at[which, side], h_s.at[which, side], h_r.at[which, side], fdev(o))
+        at = pl.ds(side * RIM, RIM)
+        return remote(src, dst.at[at], h_s.at[which, side], h_r.at[which, side], fdev(o))
+
+    def post(src, dst, s, r, i):
+        return remote(src, dst.at[z], s.at[i], r.at[z], (f, zrel(i)))
+
+    def posted(src, dst, s, r, i):
+        origin = zrel(i)
+        return remote(src, dst.at[origin], s.at[i], r.at[origin], (f, origin))
 
     def weight(i):
         there = zrel(i)
         return remote(w_ref.at[:, part(there)], wcol.at[z], w_s.at[i], w_r.at[z], (f, there))
 
-    def hop(buf, s, r, way, k, arrived=False):
-        back = k if arrived else k - 1
-        origin = zrel(-back if way == 0 else back)
-        half = width // 2
-        at = part(origin) if k < HOPS else part(origin, half, half * way)
-        return remote(
-            buf.at[at], buf.at[at], s.at[way, k - 1], r.at[way, k - 1], (f, zrel(1 if way == 0 else -1))
-        )
-
-    def pass_on(buf, s, r, k):
-        for way in range(2):
-            if k > 1:
-                hop(buf, s, r, way, k - 1, True).wait_recv()
-            hop(buf, s, r, way, k).start()
+    HOPS = ((0, 2), (0, -2), (0, 1), (0, -1), (-2, 1), (2, -1), (-2, 2), (2, -2))
+
+    def hop(buf, s, r, n, arrived=False):
+        origin, target = HOPS[n]
+        slot = zrel(origin - target if arrived else origin)
+        block = buf.at[slot]
+        if n >= 6:
+            half = buf.shape[1] // 2
+            block = buf.at[slot, pl.ds(half * (n - 6), half)]
+        return remote(block, block, s.at[n], r.at[n], (f, zrel(target)))
+
+    def hops(buf, s, r, which):
+        for n in which:
+            hop(buf, s, r, n).start()
+
+    def arrive(buf, s, r, which):
+        for n in which:
+            hop(buf, s, r, n, True).wait_recv()
 
     def penalty(query_block, key_block):
         inside = (query_block >= 0) & (query_block < frames) & (key_block >= 0) & (key_block < frames)
         safe = lax.rem(query_block + frames, frames)
         number = cnt_ref[0, safe]
         hit = False
-        for entry in range(pat_ref.shape[2]):
-            hit = hit | ((pat_ref[0, safe, entry] == key_block) & (entry < number))
+        for entry in range(pat_ref.shape[0]):
+            hit = hit | ((pat_ref[entry, 0, safe] == key_block) & (entry < number))
         return jnp.where(inside & hit, 0.0, HUGE)
 
-    def conv(src, which, flip, out):
-        pad[RIM : RIM + rows, :] = src[...].astype(jnp.float32)
-        for o in (1, -1):
-            edge(src, which, o).wait_recv()
-        left = halo[which, 0].astype(jnp.float32)
-        right = halo[which, 1].astype(jnp.float32)
-        pad[0:RIM, :] = jnp.where(f > 0, left, 0.0)
-        pad[RIM + rows : 2 * RIM + rows, :] = jnp.where(f < frames - 1, right, 0.0)
+    def conv(left, right, flip, out):
+        pad[0:RIM, :] = jnp.where(f > 0, left.astype(jnp.float32), 0.0)
+        pad[RIM + rows : 2 * RIM + rows, :] = jnp.where(f < frames - 1, right.astype(jnp.float32), 0.0)
         step = 64
         for c in range(rows // step):
             total_c = jnp.zeros((step, width), jnp.float32)
@@ -211,6 +219,12 @@
                 tap = KERNEL - 1 - t if flip else t
                 total_c = total_c + taps[tap : tap + 1, :] * pad[c * step + t + 1 : c * step + t + 1 + step, :]
             out[c * step : c * step + step, :] = total_c.astype(jnp.bfloat16)
+
+    def conv_group(group):
+        pad[RIM : RIM + rows, :] = g_all[group].astype(jnp.float32)
+        taps[...] = mail_all[group, 2 * RIM : MAIL, :].astype(jnp.float32)
+        conv(mail_all[group, 0:RIM, :], mail_all[group, RIM : 2 * RIM, :], True, conv_tmp)
+        grad_acc[...] += dot(w_ref[:, part(group)], conv_tmp[...], NT)
 
     def head_columns(x, dst):
         dst[0:HEAD_DIM, 0:rows] = x[0:HEAD_DIM, :]
@@ -302,30 +316,42 @@
             gk_acc[at, :] = gk
 
     loads[0].wait()
-    go_t[...] = g_ref[...].T
+    g_all[z] = g_ref[...].T
     loads[1].wait()
     loads[2].wait()
     pl.semaphore_wait(barrier, SPAN - 1 + heads - 1)
+
+    def grad_edge(o):
+        src = g_all.at[z, pl.ds(rows - RIM if o == 1 else 0, RIM)]
+        return edge(src, mail, 0, o)
+
     for o in (1, -1):
-        edge(go_t, 0, o).start()
+        grad_edge(o).start()
+    hops(g_all, g_s, g_r, range(4))
     for role in FIRST:
         route(kv, kv_s, kv_r, role).start()
-    loads[5].wait()
-    for i in range(1, heads):
-        weight(i).start()
     loads[3].wait()
-    loads[4].wait()
-    taps[0:KERNEL, :] = t_ref[...].astype(jnp.float32)
     qs[OWN] = (qs[OWN].astype(jnp.float32) * HEAD_DIM**-0.5).astype(jnp.bfloat16)
     head_columns(qs[OWN].T, qmt)
-
-    conv(go_t, 0, True, conv_tmp)
-    gm_all[part(z), :] = conv_tmp[...].T
-    pass_on(gm_all, gm_s, gm_r, 1)
-
+    loads[4].wait()
+    mail[2 * RIM : MAIL - 1, :] = t_ref[...]
+    mail[MAIL - 1 : MAIL, :] = jnp.zeros((1, width), jnp.bfloat16)
+    loads[5].wait()
+    grad_acc[...] = jnp.zeros_like(grad_acc)
     forward(0)
+
+    for o in (1, -1):
+        grad_edge(o).wait_recv()
+    for i in range(1, heads):
+        post(mail, mail_all, m_s, m_r, i).start()
+    mail_all[z] = mail[...]
     route(kv, kv_s, kv_r, PAIR).wait_recv()
     forward(1)
+    head_rows(kv[OWN, 0], km)
+    head_rows(kv[OWN, 1], vm)
+    conv_group(z)
+    arrive(g_all, g_s, g_r, (0, 1))
+    hops(g_all, g_s, g_r, (4, 5, 6, 7))
     route(kv, kv_s, kv_r, UP).wait_recv()
     route(kv, kv_s, kv_r, DOWN).wait_recv()
     for role in SECOND:
@@ -333,72 +359,89 @@
     for role in FIRST:
         route(qs, q_s, q_r, role).start()
     forward(2)
-    pass_on(gm_all, gm_s, gm_r, 2)
-    route(kv, kv_s, kv_r, PAIR_UP).wait_recv()
-    route(kv, kv_s, kv_r, PAIR_DOWN).wait_recv()
+    for i in range(1, heads):
+        weight(i).start()
+    for role in SECOND:
+        route(kv, kv_s, kv_r, role).wait_recv()
     forward(3)
     route(kv, kv_s, kv_r, FAR).wait_recv()
     forward(4)
 
     attended = (acc[...] * by_head(1.0 / total[...])).astype(jnp.bfloat16)
-    at_all[part(z), :] = attended
-    pass_on(gm_all, gm_s, gm_r, 3)
-    pass_on(at_all, at_s, at_r, 1)
-
-    head_rows(kv[OWN, 0], km)
-    head_rows(kv[OWN, 1], vm)
-    for role in range(SPAN):
-        kt[role] = kv[role, 0].T
+    at_all[z] = attended
+    hops(at_all, at_s, at_r, range(4))
+    by_frame = attended.T
+    ends[0:RIM, :] = by_frame[rows - RIM : rows, :]
+    ends[RIM : 2 * RIM, :] = by_frame[0:RIM, :]
+
+    def attended_edge(o):
+        return edge(ends.at[pl.ds(0 if o == 1 else RIM, RIM)], rim, 1, o)
+
+    for o in (1, -1):
+        attended_edge(o).start()
     logsum = peak[...] + jnp.log(total[...])
     stats[OWN, 0:1, :] = logsum[:, 0:rows]
     stats[OWN, 1:2, :] = logsum[:, rows : 2 * rows]
     stats[OWN, 4:8, :] = jnp.zeros((4, rows), jnp.float32)
-    wcol[z] = w_ref[:, part(z)]
-    route(qs, q_s, q_r, UP).wait_recv()
-    route(qs, q_s, q_r, DOWN).wait_recv()
+
+    arrive(g_all, g_s, g_r, (2, 3))
+    for i in range(1, heads):
+        posted(mail, mail_all, m_s, m_r, i).wait_recv()
+
+    def near_groups(i, carry):
+        conv_group(zrel(i - 2 + i // 2))
+        return carry
+
+    lax.fori_loop(0, 4, near_groups, 0)
+    for role in (UP, DOWN):
+        route(qs, q_s, q_r, role).wait_recv()
     for role in SECOND:
         route(qs, q_s, q_r, role).start()
-    pass_on(gm_all, gm_s, gm_r, 4)
-    for i in range(1, heads):
-        src = zrel(i)
-        remote(w_ref.at[:, part(z)], wcol.at[src], w_s.at[i], w_r.at[src], (f, src)).wait_recv()
-    for i in range(heads):
-        wcol_t[:, i * width : (i + 1) * width] = wcol[i].T
-    for way in range(2):
-        hop(gm_all, gm_s, gm_r, way, HOPS, True).wait_recv()
-
-    grad_t = dot(w_ref[...], gm_all[...], NN).astype(jnp.bfloat16)
+    for o in (1, -1):
+        attended_edge(o).wait_recv()
+    for i in range(1, heads):
+        post(rim, rim_all, e_s, e_r, i).start()
+    rim_all[z] = rim[...]
+    for role in range(SPAN):
+        kt[role] = kv[role, 0].T
+    arrive(g_all, g_s, g_r, (4, 5, 6, 7))
+
+    def far_groups(i, carry):
+        conv_group(zrel(i + 3))
+        return carry
+
+    lax.fori_loop(0, 3, far_groups, 0)
+
+    grad_t = grad_acc[...].astype(jnp.bfloat16)
     do[OWN] = grad_t.T
     for role in FIRST:
         route(do, do_s, do_r, role).start()
-    product = grad_t.astype(jnp.float32) * attended.astype(jnp.float32)
+    product = grad_t.astype(jnp.float32) * at_all[z].astype(jnp.float32)
     stats[OWN, 2:3, :] = jnp.sum(product[0:HEAD_DIM, :], axis=0, keepdims=True)
     stats[OWN, 3:4, :] = jnp.sum(product[HEAD_DIM:width, :], axis=0, keepdims=True)
     for role in range(1, SPAN):
         direct(role).start()
     head_columns(grad_t, dmt)
 
-    pass_on(at_all, at_s, at_r, 2)
+    arrive(at_all, at_s, at_r, (0, 1))
+    hops(at_all, at_s, at_r, (4, 5, 6, 7))
     back_queries(0)
-    pass_on(at_all, at_s, at_r, 3)
-    route(do, do_s, do_r, UP).wait_recv()
-    route(do, do_s, do_r, DOWN).wait_recv()
+    wcol[z] = w_ref[:, part(z)]
+    for i in range(1, heads):
+        src = zrel(i)
+        remote(w_ref.at[:, part(z)], wcol.at[src], w_s.at[i], w_r.at[src], (f, src)).wait_recv()
+    for i in range(heads):
+        wcol_t[:, i * width : (i + 1) * width] = wcol[i].T
+    back_queries(1)
+    dq_ref[...] = acc[...].T.astype(jnp.bfloat16)
+    for role in (UP, DOWN):
+        route(do, do_s, do_r, role).wait_recv()
     for role in SECOND:
         route(do, do_s, do_r, role).start()
-    back_queries(1)
-    dq_ref[...] = acc[...].T.astype(jnp.bfloat16)
-    stores = [
-        pltpu.make_async_copy(src, dst, out_s.at[n])
-        for n, (src, dst) in enumerate(
-            ((dq_ref, dq_hbm), (dk_ref, dk_hbm), (dv_ref, dv_hbm), (co_ref, co_hbm))
-        )
-    ]
-    stores[0].start()
-    pass_on(at_all, at_s, at_r, 4)
     back_keys(OWN)
 
     def keys_of(role):
-        if role in (PAIR, PAIR_UP, PAIR_DOWN, FAR):
+        if role not in (UP, DOWN):
             route(qs, q_s, q_r, role).wait_recv()
             route(do, do_s, do_r, role).wait_recv()
         direct(role).wait_recv()
@@ -407,28 +450,29 @@
     keys_of(PAIR)
     keys_of(UP)
     keys_of(DOWN)
-
-    for way in range(2):
-        hop(at_all, at_s, at_r, way, HOPS, True).wait_recv()
-    mixed[...] = dot(wcol_t[...], at_all[...], NN).T.astype(jnp.bfloat16)
-    for o in (1, -1):
-        edge(mixed, 1, o).start()
-
     keys_of(PAIR_UP)
     keys_of(PAIR_DOWN)
     keys_of(FAR)
     dv_ref[...] = jnp.where(low, gv_acc[0:rows, :], gv_acc[rows : 2 * rows, :]).astype(jnp.bfloat16)
     dk_ref[...] = jnp.where(low, gk_acc[0:rows, :], gk_acc[rows : 2 * rows, :]).astype(jnp.bfloat16)
-    stores[1].start()
-    stores[2].start()
-
-    conv(mixed, 1, False, conv_tmp)
+
+    for i in range(1, heads):
+        posted(rim, rim_all, e_s, e_r, i).wait_recv()
+    arrive(at_all, at_s, at_r, range(2, len(HOPS)))
+    side = jnp.zeros((2 * RIM, width), jnp.float32)
+    for i in range(heads):
+        side = side + dot(rim_all[i], wcol[i], NN)
+    side = side.astype(jnp.bfloat16)
+    gathered = at_all[...].reshape(heads * width, rows)
+    mixed = dot(wcol_t[...], gathered, NN).T.astype(jnp.bfloat16)
+    pad[RIM : RIM + rows, :] = mixed.astype(jnp.float32)
+    taps[...] = mail_all[z, 2 * RIM : MAIL, :].astype(jnp.float32)
+    conv(side[0:RIM, :], side[RIM : 2 * RIM, :], False, conv_tmp)
     co_ref[...] = conv_tmp[...].T
-    stores[3].start()
 
     for o in (1, -1):
-        edge(go_t, 0, o).wait_send()
-        edge(mixed, 1, o).wait_send()
+        grad_edge(o).wait_send()
+        attended_edge(o).wait_send()
     for role in range(1, SPAN):
         route(kv, kv_s, kv_r, role).wait_send()
         route(qs, q_s, q_r, role).wait_send()
@@ -436,12 +480,23 @@
         direct(role).wait_send()
     for i in range(1, heads):
         weight(i).wait_send()
-    for k in range(1, HOPS + 1):
-        for way in range(2):
-            hop(gm_all, gm_s, gm_r, way, k).wait_send()
-            hop(at_all, at_s, at_r, way, k).wait_send()
-    for store in stores:
-        store.wait()
+        post(mail, mail_all, m_s, m_r, i).wait_send()
+        post(rim, rim_all, e_s, e_r, i).wait_send()
+    for n in range(len(HOPS)):
+        hop(g_all, g_s, g_r, n).wait_send()
+        hop(at_all, at_s, at_r, n).wait_send()
+
+
+def copy_out(*refs):
+    half = len(refs) // 2
+    sources, targets, sems = refs[:half], refs[half : 2 * half], refs[-1]
+    copies = [
+        pltpu.make_async_copy(src, dst, sems.at[n]) for n, (src, dst) in enumerate(zip(sources, targets))
+    ]
+    for copy in copies:
+        copy.start()
+    for copy in copies:
+        copy.wait()
 
 
 def on_device(queries, keys, values, out_weight, conv_kernel, grad_out, pattern, counts):
@@ -452,40 +507,41 @@
     hbm = pl.BlockSpec(memory_space=pltpu.HBM)
     smem = pl.BlockSpec(memory_space=pltpu.SMEM)
     dma = pltpu.SemaphoreType.DMA
-    conv_out, dq, dk, dv = pl.pallas_call(
+    vmem = pl.BlockSpec(memory_space=pltpu.VMEM)
+    shapes = [
+        jax.ShapeDtypeStruct(tall, bf),
+        jax.ShapeDtypeStruct(block, bf),
+        jax.ShapeDtypeStruct(block, bf),
+        jax.ShapeDtypeStruct(block, bf),
+    ]
+    results = pl.pallas_call(
         partial(kernel, frames, heads),
-        out_shape=[
-            jax.ShapeDtypeStruct(tall, bf),
-            jax.ShapeDtypeStruct(block, bf),
-            jax.ShapeDtypeStruct(block, bf),
-            jax.ShapeDtypeStruct(block, bf),
-        ],
+        out_shape=shapes,
         in_specs=[hbm] * 6 + [smem] * 2,
-        out_specs=[hbm] * 4,
+        out_specs=[vmem] * 4,
         scratch_shapes=[
             pltpu.VMEM(out_weight.shape, bf),
             pltpu.VMEM(conv_kernel.shape, bf),
             pltpu.VMEM(tall, bf),
-            pltpu.VMEM(tall, bf),
-            pltpu.VMEM(block, bf),
-            pltpu.VMEM(block, bf),
-            pltpu.VMEM(block, bf),
             pltpu.VMEM((SPAN, 2) + block, bf),
             pltpu.VMEM((SPAN,) + tall, bf),
             pltpu.VMEM((SPAN,) + tall, bf),
             pltpu.VMEM((SPAN,) + block, bf),
             pltpu.VMEM((SPAN,) + block, bf),
             pltpu.VMEM((SPAN, 8, rows), f32),
-            pltpu.VMEM((heads * width, rows), bf),
-            pltpu.VMEM((heads * width, rows), bf),
+            pltpu.VMEM((heads,) + block, bf),
+            pltpu.VMEM((heads,) + tall, bf),
+            pltpu.VMEM((MAIL, width), bf),
+            pltpu.VMEM((heads, MAIL, width), bf),
+            pltpu.VMEM((2 * RIM, width), bf),
+            pltpu.VMEM((2 * RIM, width), bf),
+            pltpu.VMEM((heads, 2 * RIM, width), bf),
             pltpu.VMEM((heads, width, width), bf),
             pltpu.VMEM((width, heads * width), bf),
             pltpu.VMEM(block, bf),
-            pltpu.VMEM(block, bf),
-            pltpu.VMEM(block, bf),
-            pltpu.VMEM((2, 2, RIM, width), bf),
             pltpu.VMEM((rows + 2 * RIM, width), f32),
-            pltpu.VMEM((32, width), f32),
+            pltpu.VMEM((2 * RIM, width), f32),
+            pltpu.VMEM(tall, f32),
             pltpu.VMEM((width, 2 * rows), bf),
             pltpu.VMEM((width, 2 * rows), bf),
             pltpu.VMEM((2 * rows, width), bf),
@@ -498,11 +554,9 @@
             pltpu.VMEM((2 * rows, width), f32),
             pltpu.VMEM((2 * rows, width), f32),
             dma((6,)),
-            dma((4,)),
         ]
         + [dma((SPAN,))] * 8
-        + [dma((heads,))] * 2
-        + [dma((2, HOPS))] * 4
+        + [dma((heads,))] * 10
         + [dma((2, 2))] * 2,
         compiler_params=pltpu.CompilerParams(
             collective_id=0, has_side_effects=True, vmem_limit_bytes=56 * 1024 * 1024
@@ -514,9 +568,16 @@
         out_weight,
         conv_kernel,
         grad_out.reshape(width, rows),
-        pattern,
+        jnp.transpose(pattern, (2, 0, 1)),
         counts,
     )
+    conv_out, dq, dk, dv = pl.pallas_call(
+        copy_out,
+        out_shape=shapes,
+        in_specs=[vmem] * 4,
+        out_specs=[hbm] * 4,
+        scratch_shapes=[dma((4,))],
+    )(*results)
     return (
         conv_out.reshape(grad_out.shape),
         dq.reshape(queries.shape),

time: 63.7 us -> 61.3 us (0.962)
  local copies, waits for them, and re-layouts: 5.53 us -> 0 us
  Pallas kernels: 56.9 us -> 60.4 us
    unnamed x13 -> x0, local copies, waits for them, and re-layouts: 5.53 us -> none
    pallas_call x1 -> x2, Pallas kernels: 56.9 us -> 60.4 us  [the longest x1 58.5 us: on_device(): pl.pallas_call(partial(kernel, frames, heads), out_shape=shapes, in_specs...]
where the time goes in v3:
time: 61.3 us; the launch traced here: 61.2 us
  Pallas kernels  60.4 us (99%)
  between operations  0.8 us (1%)
    pallas_call x1, Pallas kernels, on_device(): pl.pallas_call(partial(kernel, frames, heads), out_shape=shapes, in_specs...  58.5 us
    pallas_call x1, Pallas kernels, on_device(): pl.pallas_call(copy_out, out_shape=shapes, in_specs=[vmem] * 4, out_specs...  1.91 us

profile of v3, /device:TPU:1, one launch (start us, length us, event | category | flops | bytes accessed | tf_op | source)
XLA Modules:
  0.0 61.2 jit_solution(13336752712117043665)
XLA Ops:
  0.6 58.5 %shard_map.111 = (bf16[128,512]{1,0:T(8,128)(2,1)}, bf16[512,128]{1,0:T(8,128)(2,1)}, bf16[512,128]{1,0:T(8,128)(2,1)}, bf16[512,128]{1,0:T(8,128)(2,1)}) custom-call(bf16[512,128]{1,0:T(8,128)(2,1)} %bitcast.9, bf16[512,128]{1,0:T(8,128)(2,1)} %bitcast.10, bf16[512,128]{1,0:T(8,128)(2,1)} %bitcast.11, bf16[128,1024]{1,0:T(8,128)(2,1)} %w_hbm.1, ...), custom_call_target="tpu_custom_call" | custom-call | tf_op jit(solution)/shard_map/pallas_call | solution.py:517
  59.1 1.9 %shard_map.112 = (bf16[128,512]{1,0:T(8,128)(2,1)}, bf16[512,128]{1,0:T(8,128)(2,1)}, bf16[512,128]{1,0:T(8,128)(2,1)}, bf16[512,128]{1,0:T(8,128)(2,1)}) custom-call(bf16[128,512]{1,0:T(8,128)(2,1)} %get-tuple-element.12.refs_0_, bf16[512,128]{1,0:T(8,128)(2,1)} %get-tuple-element.13.refs_1_, bf16[512,128]{1,0:T(8,128)(2,1)} %get-tuple-element.14.refs_2_, ...), custom_call_target="tpu_custom_call" | custom-call | tf_op jit(solution)/shard_map/pallas_call | solution.py:574

commit v4 on v3

--- a/solution.py
+++ b/solution.py
@@ -14,6 +14,7 @@
 MESH = pl.DeviceIdType.MESH
 RIM = 16
 MAIL = 64
+QUARTERS = 4
 
 NT = (((1,), (1,)), ((), ()))
 NN = (((1,), (0,)), ((), ()))
@@ -43,6 +44,10 @@
     g_hbm,
     pat_ref,
     cnt_ref,
+    co_hbm,
+    dq_hbm,
+    dk_hbm,
+    dv_hbm,
     co_ref,
     dq_ref,
     dk_ref,
@@ -63,6 +68,7 @@
     ends,
     rim,
     rim_all,
+    side_ref,
     wcol,
     wcol_t,
     conv_tmp,
@@ -74,6 +80,7 @@
     km,
     vm,
     probs,
+    key_probs,
     peaks,
     peak,
     total,
@@ -81,6 +88,7 @@
     gk_acc,
     gv_acc,
     in_s,
+    out_s,
     kv_s,
     kv_r,
     q_s,
@@ -91,6 +99,8 @@
     st_r,
     w_s,
     w_r,
+    x_s,
+    x_r,
     g_s,
     g_r,
     at_s,
@@ -140,13 +150,15 @@
         pl.semaphore_signal(barrier, inc=1, device_id=fdev(o), device_id_type=MESH)
     for i in range(1, heads):
         pl.semaphore_signal(barrier, inc=1, device_id=(f, zrel(i)), device_id_type=MESH)
+    for d in range(1, QUARTERS):
+        pl.semaphore_signal(barrier, inc=1, device_id=fdev(d * (frames // QUARTERS)), device_id_type=MESH)
 
     def route(buf, s, r, role):
         src, o = {
             PAIR: (OWN, -sign),
             DOWN: (OWN, 2),
             UP: (OWN, -2),
-            FAR: (OWN, 3 * sign),
+            FAR: (UP + odd, sign) if buf is kv else (OWN, 3 * sign),
             PAIR_UP: (UP, -sign),
             PAIR_DOWN: (DOWN, -sign),
         }[role]
@@ -154,7 +166,7 @@
 
     FIRST, SECOND = (UP, DOWN, PAIR, FAR), (PAIR_UP, PAIR_DOWN)
 
-    def direct(role):
+    def direct(role, which):
         o = {
             PAIR: -sign,
             DOWN: 2,
@@ -163,7 +175,10 @@
             PAIR_UP: -2 - sign,
             FAR: 3 * sign,
         }[role]
-        return remote(stats.at[OWN], stats.at[role], st_s.at[role], st_r.at[role], fdev(o))
+        at = pl.ds(8 * which, 8)
+        return remote(
+            stats.at[OWN, at], stats.at[role, at], st_s.at[which, role], st_r.at[which, role], fdev(o)
+        )
 
     def edge(src, dst, which, o):
         side = 0 if o == 1 else 1
@@ -177,9 +192,19 @@
         origin = zrel(i)
         return remote(src, dst.at[origin], s.at[i], r.at[origin], (f, origin))
 
-    def weight(i):
+    stride, share = frames // QUARTERS, width // QUARTERS
+    own_rows = pl.ds(pl.multiple_of((f // stride) * share, share), share)
+
+    def weight(i, arrived=False):
         there = zrel(i)
-        return remote(w_ref.at[:, part(there)], wcol.at[z], w_s.at[i], w_r.at[z], (f, there))
+        if arrived:
+            return remote(wcol.at[there, own_rows], wcol.at[there, own_rows], w_s.at[i], w_r.at[there], (f, there))
+        return remote(w_ref.at[own_rows, part(there)], wcol.at[z, own_rows], w_s.at[i], w_r.at[z], (f, there))
+
+    def quarter(d, arrived=False):
+        back = lax.rem(f // stride + QUARTERS - d, QUARTERS) if arrived else f // stride
+        at = pl.ds(pl.multiple_of(back * share, share), share)
+        return remote(wcol.at[:, at], wcol.at[:, at], x_s.at[d], x_r.at[d], fdev(d * stride))
 
     HOPS = ((0, 2), (0, -2), (0, 1), (0, -1), (-2, 1), (2, -1), (-2, 2), (2, -2))
 
@@ -290,7 +315,7 @@
         feats = slice(h * HEAD_DIM, (h + 1) * HEAD_DIM)
         out = jnp.zeros((HEAD_DIM, rows), jnp.float32)
         factor = HEAD_DIM**-0.5 / total[:, cols]
-        delta = stats[OWN, 2 + h : 3 + h, :]
+        delta = stats[OWN, 8 + h : 9 + h, :]
         for group, roles in enumerate(GROUPS):
             scale = factor * jnp.exp(peaks[group, :, cols] - peak[:, cols])
             for role in roles:
@@ -299,15 +324,20 @@
                 out = out + scale * dot(kt[role, feats, :], ds, NN)
         acc[feats, :] = out
 
-    def back_keys(role):
+    def key_weights(role):
         pen = penalty(f + offsets[role], f)
         for h in range(2):
             at = slice(h * rows, h * rows + rows)
             st = dot(km[at, :], qs[role], NT)
-            pt = jnp.exp(st - (stats[role, h : h + 1, :] + pen))
+            key_probs[role, at, :] = jnp.exp(st - (stats[role, h : h + 1, :] + pen)).astype(jnp.bfloat16)
+
+    def back_keys(role):
+        for h in range(2):
+            at = slice(h * rows, h * rows + rows)
+            pt = key_probs[role, at, :]
             dpt = dot(vm[at, :], do[role], NT)
-            dst = (pt * (dpt - stats[role, 2 + h : 3 + h, :])).astype(jnp.bfloat16)
-            gv = dot(pt.astype(jnp.bfloat16), do[role], NN)
+            dst = (pt.astype(jnp.float32) * (dpt - stats[role, 8 + h : 9 + h, :])).astype(jnp.bfloat16)
+            gv = dot(pt, do[role], NN)
             gk = dot(dst, qs[role], NN)
             if role != OWN:
                 gv = gv + gv_acc[at, :]
@@ -319,7 +349,7 @@
     g_all[z] = g_ref[...].T
     loads[1].wait()
     loads[2].wait()
-    pl.semaphore_wait(barrier, SPAN - 1 + heads - 1)
+    pl.semaphore_wait(barrier, SPAN - 1 + heads - 1 + QUARTERS - 1)
 
     def grad_edge(o):
         src = g_all.at[z, pl.ds(rows - RIM if o == 1 else 0, RIM)]
@@ -327,8 +357,8 @@
 
     for o in (1, -1):
         grad_edge(o).start()
-    hops(g_all, g_s, g_r, range(4))
-    for role in FIRST:
+    hops(g_all, g_s, g_r, (0, 1))
+    for role in (UP, DOWN, PAIR):
         route(kv, kv_s, kv_r, role).start()
     loads[3].wait()
     qs[OWN] = (qs[OWN].astype(jnp.float32) * HEAD_DIM**-0.5).astype(jnp.bfloat16)
@@ -337,6 +367,9 @@
     mail[2 * RIM : MAIL - 1, :] = t_ref[...]
     mail[MAIL - 1 : MAIL, :] = jnp.zeros((1, width), jnp.bfloat16)
     loads[5].wait()
+    for i in range(1, heads):
+        weight(i).start()
+    wcol[z, own_rows] = w_ref[own_rows, part(z)]
     grad_acc[...] = jnp.zeros_like(grad_acc)
     forward(0)
 
@@ -346,6 +379,7 @@
         post(mail, mail_all, m_s, m_r, i).start()
     mail_all[z] = mail[...]
     route(kv, kv_s, kv_r, PAIR).wait_recv()
+    hops(g_all, g_s, g_r, (2, 3))
     forward(1)
     head_rows(kv[OWN, 0], km)
     head_rows(kv[OWN, 1], vm)
@@ -354,13 +388,15 @@
     hops(g_all, g_s, g_r, (4, 5, 6, 7))
     route(kv, kv_s, kv_r, UP).wait_recv()
     route(kv, kv_s, kv_r, DOWN).wait_recv()
-    for role in SECOND:
+    for role in (FAR,) + SECOND:
         route(kv, kv_s, kv_r, role).start()
     for role in FIRST:
         route(qs, q_s, q_r, role).start()
     forward(2)
     for i in range(1, heads):
-        weight(i).start()
+        weight(i, True).wait_recv()
+    for d in range(1, QUARTERS):
+        quarter(d).start()
     for role in SECOND:
         route(kv, kv_s, kv_r, role).wait_recv()
     forward(3)
@@ -369,7 +405,7 @@
 
     attended = (acc[...] * by_head(1.0 / total[...])).astype(jnp.bfloat16)
     at_all[z] = attended
-    hops(at_all, at_s, at_r, range(4))
+    hops(at_all, at_s, at_r, (0, 1))
     by_frame = attended.T
     ends[0:RIM, :] = by_frame[rows - RIM : rows, :]
     ends[RIM : 2 * RIM, :] = by_frame[0:RIM, :]
@@ -382,7 +418,9 @@
     logsum = peak[...] + jnp.log(total[...])
     stats[OWN, 0:1, :] = logsum[:, 0:rows]
     stats[OWN, 1:2, :] = logsum[:, rows : 2 * rows]
-    stats[OWN, 4:8, :] = jnp.zeros((4, rows), jnp.float32)
+    stats[OWN, 2:8, :] = jnp.zeros((6, rows), jnp.float32)
+    for role in range(1, SPAN):
+        direct(role, 0).start()
 
     arrive(g_all, g_s, g_r, (2, 3))
     for i in range(1, heads):
@@ -393,17 +431,18 @@
         return carry
 
     lax.fori_loop(0, 4, near_groups, 0)
+    hops(at_all, at_s, at_r, (2, 3))
     for role in (UP, DOWN):
         route(qs, q_s, q_r, role).wait_recv()
     for role in SECOND:
         route(qs, q_s, q_r, role).start()
-    for o in (1, -1):
-        attended_edge(o).wait_recv()
-    for i in range(1, heads):
-        post(rim, rim_all, e_s, e_r, i).start()
-    rim_all[z] = rim[...]
+    key_weights(OWN)
     for role in range(SPAN):
         kt[role] = kv[role, 0].T
+    for d in range(1, QUARTERS):
+        quarter(d, True).wait_recv()
+    for i in range(heads):
+        wcol_t[:, i * width : (i + 1) * width] = wcol[i].T
     arrive(g_all, g_s, g_r, (4, 5, 6, 7))
 
     def far_groups(i, carry):
@@ -417,34 +456,60 @@
     for role in FIRST:
         route(do, do_s, do_r, role).start()
     product = grad_t.astype(jnp.float32) * at_all[z].astype(jnp.float32)
-    stats[OWN, 2:3, :] = jnp.sum(product[0:HEAD_DIM, :], axis=0, keepdims=True)
-    stats[OWN, 3:4, :] = jnp.sum(product[HEAD_DIM:width, :], axis=0, keepdims=True)
+    stats[OWN, 8:9, :] = jnp.sum(product[0:HEAD_DIM, :], axis=0, keepdims=True)
+    stats[OWN, 9:10, :] = jnp.sum(product[HEAD_DIM:width, :], axis=0, keepdims=True)
+    stats[OWN, 10:16, :] = jnp.zeros((6, rows), jnp.float32)
     for role in range(1, SPAN):
-        direct(role).start()
+        direct(role, 1).start()
     head_columns(grad_t, dmt)
 
+    def ready(role):
+        if role not in (OWN, UP, DOWN):
+            route(qs, q_s, q_r, role).wait_recv()
+        if role != OWN:
+            direct(role, 0).wait_recv()
+        key_weights(role)
+
+    back_queries(0)
+    for o in (1, -1):
+        attended_edge(o).wait_recv()
+    for i in range(1, heads):
+        post(rim, rim_all, e_s, e_r, i).start()
+    rim_all[z] = rim[...]
+    back_queries(1)
+    dq_ref[...] = acc[...].T.astype(jnp.bfloat16)
+    stores = [
+        pltpu.make_async_copy(src, dst, out_s.at[n])
+        for n, (src, dst) in enumerate(
+            ((dq_ref, dq_hbm), (dk_ref, dk_hbm), (dv_ref, dv_hbm), (co_ref, co_hbm))
+        )
+    ]
+    stores[0].start()
+    ready(PAIR)
     arrive(at_all, at_s, at_r, (0, 1))
     hops(at_all, at_s, at_r, (4, 5, 6, 7))
-    back_queries(0)
-    wcol[z] = w_ref[:, part(z)]
-    for i in range(1, heads):
-        src = zrel(i)
-        remote(w_ref.at[:, part(z)], wcol.at[src], w_s.at[i], w_r.at[src], (f, src)).wait_recv()
-    for i in range(heads):
-        wcol_t[:, i * width : (i + 1) * width] = wcol[i].T
-    back_queries(1)
-    dq_ref[...] = acc[...].T.astype(jnp.bfloat16)
+    ready(UP)
+    ready(DOWN)
     for role in (UP, DOWN):
         route(do, do_s, do_r, role).wait_recv()
     for role in SECOND:
         route(do, do_s, do_r, role).start()
+    ready(PAIR_UP)
+    ready(PAIR_DOWN)
+    ready(FAR)
     back_keys(OWN)
+    for i in range(1, heads):
+        posted(rim, rim_all, e_s, e_r, i).wait_recv()
+    side = jnp.zeros((2 * RIM, width), jnp.float32)
+    for i in range(heads):
+        side = side + dot(rim_all[i], wcol[i], NN)
+    side_ref[...] = side.astype(jnp.bfloat16)
+    taps[...] = mail_all[z, 2 * RIM : MAIL, :].astype(jnp.float32)
 
     def keys_of(role):
         if role not in (UP, DOWN):
-            route(qs, q_s, q_r, role).wait_recv()
             route(do, do_s, do_r, role).wait_recv()
-        direct(role).wait_recv()
+        direct(role, 1).wait_recv()
         back_keys(role)
 
     keys_of(PAIR)
@@ -455,20 +520,16 @@
     keys_of(FAR)
     dv_ref[...] = jnp.where(low, gv_acc[0:rows, :], gv_acc[rows : 2 * rows, :]).astype(jnp.bfloat16)
     dk_ref[...] = jnp.where(low, gk_acc[0:rows, :], gk_acc[rows : 2 * rows, :]).astype(jnp.bfloat16)
-
-    for i in range(1, heads):
-        posted(rim, rim_all, e_s, e_r, i).wait_recv()
+    stores[1].start()
+    stores[2].start()
+
     arrive(at_all, at_s, at_r, range(2, len(HOPS)))
-    side = jnp.zeros((2 * RIM, width), jnp.float32)
-    for i in range(heads):
-        side = side + dot(rim_all[i], wcol[i], NN)
-    side = side.astype(jnp.bfloat16)
     gathered = at_all[...].reshape(heads * width, rows)
     mixed = dot(wcol_t[...], gathered, NN).T.astype(jnp.bfloat16)
     pad[RIM : RIM + rows, :] = mixed.astype(jnp.float32)
-    taps[...] = mail_all[z, 2 * RIM : MAIL, :].astype(jnp.float32)
-    conv(side[0:RIM, :], side[RIM : 2 * RIM, :], False, conv_tmp)
+    conv(side_ref[0:RIM, :], side_ref[RIM : 2 * RIM, :], False, conv_tmp)
     co_ref[...] = conv_tmp[...].T
+    stores[3].start()
 
     for o in (1, -1):
         grad_edge(o).wait_send()
@@ -477,14 +538,19 @@
         route(kv, kv_s, kv_r, role).wait_send()
         route(qs, q_s, q_r, role).wait_send()
         route(do, do_s, do_r, role).wait_send()
-        direct(role).wait_send()
+        direct(role, 0).wait_send()
+        direct(role, 1).wait_send()
     for i in range(1, heads):
         weight(i).wait_send()
         post(mail, mail_all, m_s, m_r, i).wait_send()
         post(rim, rim_all, e_s, e_r, i).wait_send()
+    for d in range(1, QUARTERS):
+        quarter(d).wait_send()
     for n in range(len(HOPS)):
         hop(g_all, g_s, g_r, n).wait_send()
         hop(at_all, at_s, at_r, n).wait_send()
+    for store in stores:
+        store.wait()
 
 
 def copy_out(*refs):
@@ -518,8 +584,12 @@
         partial(kernel, frames, heads),
         out_shape=shapes,
         in_specs=[hbm] * 6 + [smem] * 2,
-        out_specs=[vmem] * 4,
+        out_specs=[hbm] * 4,
         scratch_shapes=[
+            pltpu.VMEM(tall, bf),
+            pltpu.VMEM(block, bf),
+            pltpu.VMEM(block, bf),
+            pltpu.VMEM(block, bf),
             pltpu.VMEM(out_weight.shape, bf),
             pltpu.VMEM(conv_kernel.shape, bf),
             pltpu.VMEM(tall, bf),
@@ -528,7 +598,7 @@
             pltpu.VMEM((SPAN,) + tall, bf),
             pltpu.VMEM((SPAN,) + block, bf),
             pltpu.VMEM((SPAN,) + block, bf),
-            pltpu.VMEM((SPAN, 8, rows), f32),
+            pltpu.VMEM((SPAN, 16, rows), f32),
             pltpu.VMEM((heads,) + block, bf),
             pltpu.VMEM((heads,) + tall, bf),
             pltpu.VMEM((MAIL, width), bf),
@@ -536,6 +606,7 @@
             pltpu.VMEM((2 * RIM, width), bf),
             pltpu.VMEM((2 * RIM, width), bf),
             pltpu.VMEM((heads, 2 * RIM, width), bf),
+            pltpu.VMEM((2 * RIM, width), bf),
             pltpu.VMEM((heads, width, width), bf),
             pltpu.VMEM((width, heads * width), bf),
             pltpu.VMEM(block, bf),
@@ -547,6 +618,7 @@
             pltpu.VMEM((2 * rows, width), bf),
             pltpu.VMEM((2 * rows, width), bf),
             pltpu.VMEM((SPAN, rows, 2 * rows), bf),
+            pltpu.VMEM((SPAN, 2 * rows, rows), bf),
             pltpu.VMEM((len(GROUPS), 1, 2 * rows), f32),
             pltpu.VMEM((1, 2 * rows), f32),
             pltpu.VMEM((1, 2 * rows), f32),
@@ -554,9 +626,13 @@
             pltpu.VMEM((2 * rows, width), f32),
             pltpu.VMEM((2 * rows, width), f32),
             dma((6,)),
+            dma((4,)),
         ]
-        + [dma((SPAN,))] * 8
-        + [dma((heads,))] * 10
+        + [dma((SPAN,))] * 6
+        + [dma((2, SPAN))] * 2
+        + [dma((heads,))] * 2
+        + [dma((QUARTERS,))] * 2
+        + [dma((heads,))] * 8
         + [dma((2, 2))] * 2,
         compiler_params=pltpu.CompilerParams(
             collective_id=0, has_side_effects=True, vmem_limit_bytes=56 * 1024 * 1024

time: 61.3 us -> 58 us (0.946)
  Pallas kernels: 60.4 us -> 57 us
    pallas_call x1, Pallas kernels: 58.5 us -> 55.1 us  [on_device(): pl.pallas_call(partial(kernel, frames, heads), out_shape=shapes, in_specs...]
where the time goes in v4:
time: 58 us; the launch traced here: 57.8 us
  Pallas kernels  57 us (98%)
  between operations  0.8 us (1%)
    pallas_call x1, Pallas kernels, on_device(): pl.pallas_call(partial(kernel, frames, heads), out_shape=shapes, in_specs...  55.1 us
    pallas_call x1, Pallas kernels, on_device(): pl.pallas_call(copy_out, out_shape=shapes, in_specs=[vmem] * 4, out_specs...  1.91 us

profile of v4, /device:TPU:1, one launch (start us, length us, event | category | flops | bytes accessed | tf_op | source)
XLA Modules:
  0.0 57.8 jit_solution(18092194002732782589)
XLA Ops:
  0.6 55.1 %shard_map.111 = (bf16[128,512]{1,0:T(8,128)(2,1)}, bf16[512,128]{1,0:T(8,128)(2,1)}, bf16[512,128]{1,0:T(8,128)(2,1)}, bf16[512,128]{1,0:T(8,128)(2,1)}) custom-call(bf16[512,128]{1,0:T(8,128)(2,1)} %bitcast.9, bf16[512,128]{1,0:T(8,128)(2,1)} %bitcast.10, bf16[512,128]{1,0:T(8,128)(2,1)} %bitcast.11, bf16[128,1024]{1,0:T(8,128)(2,1)} %w_hbm.1, ...), custom_call_target="tpu_custom_call" | custom-call | tf_op jit(solution)/shard_map/pallas_call | solution.py:583
  55.8 1.9 %shard_map.112 = (bf16[128,512]{1,0:T(8,128)(2,1)}, bf16[512,128]{1,0:T(8,128)(2,1)}, bf16[512,128]{1,0:T(8,128)(2,1)}, bf16[512,128]{1,0:T(8,128)(2,1)}) custom-call(bf16[128,512]{1,0:T(8,128)(2,1)} %get-tuple-element.12.refs_0_, bf16[512,128]{1,0:T(8,128)(2,1)} %get-tuple-element.13.refs_1_, bf16[512,128]{1,0:T(8,128)(2,1)} %get-tuple-element.14.refs_2_, ...), custom_call_target="tpu_custom_call" | custom-call | tf_op jit(solution)/shard_map/pallas_call | solution.py:650

commit v5 on v4

--- a/solution.py
+++ b/solution.py
@@ -42,8 +42,8 @@
     w_hbm,
     t_hbm,
     g_hbm,
-    pat_ref,
-    cnt_ref,
+    pat_hbm,
+    cnt_hbm,
     co_hbm,
     dq_hbm,
     dk_hbm,
@@ -55,6 +55,8 @@
     w_ref,
     t_ref,
     g_ref,
+    pat_ref,
+    cnt_ref,
     kv,
     kt,
     vt,
@@ -129,6 +131,14 @@
 
     offsets = (0, -sign, 2, -2, 2 - sign, -2 - sign, 3 * sign)
 
+    barrier = pltpu.get_barrier_semaphore()
+    for o in offsets[1:]:
+        pl.semaphore_signal(barrier, inc=1, device_id=fdev(o), device_id_type=MESH)
+    for i in range(1, heads):
+        pl.semaphore_signal(barrier, inc=1, device_id=(f, zrel(i)), device_id_type=MESH)
+    for d in range(1, QUARTERS):
+        pl.semaphore_signal(barrier, inc=1, device_id=fdev(d * (frames // QUARTERS)), device_id_type=MESH)
+
     loads = [
         pltpu.make_async_copy(src, dst, in_s.at[n])
         for n, (src, dst) in enumerate(
@@ -139,19 +149,13 @@
                 (q_hbm, qs.at[OWN]),
                 (t_hbm, t_ref),
                 (w_hbm, w_ref),
+                (pat_hbm, pat_ref),
+                (cnt_hbm, cnt_ref),
             )
         )
     ]
     for load in loads:
         load.start()
-
-    barrier = pltpu.get_barrier_semaphore()
-    for o in offsets[1:]:
-        pl.semaphore_signal(barrier, inc=1, device_id=fdev(o), device_id_type=MESH)
-    for i in range(1, heads):
-        pl.semaphore_signal(barrier, inc=1, device_id=(f, zrel(i)), device_id_type=MESH)
-    for d in range(1, QUARTERS):
-        pl.semaphore_signal(barrier, inc=1, device_id=fdev(d * (frames // QUARTERS)), device_id_type=MESH)
 
     def route(buf, s, r, role):
         src, o = {
@@ -371,6 +375,8 @@
         weight(i).start()
     wcol[z, own_rows] = w_ref[own_rows, part(z)]
     grad_acc[...] = jnp.zeros_like(grad_acc)
+    loads[6].wait()
+    loads[7].wait()
     forward(0)
 
     for o in (1, -1):
@@ -571,7 +577,6 @@
     bf, f32 = jnp.bfloat16, jnp.float32
     block, tall = (rows, width), (width, rows)
     hbm = pl.BlockSpec(memory_space=pltpu.HBM)
-    smem = pl.BlockSpec(memory_space=pltpu.SMEM)
     dma = pltpu.SemaphoreType.DMA
     vmem = pl.BlockSpec(memory_space=pltpu.VMEM)
     shapes = [
@@ -583,7 +588,7 @@
     results = pl.pallas_call(
         partial(kernel, frames, heads),
         out_shape=shapes,
-        in_specs=[hbm] * 6 + [smem] * 2,
+        in_specs=[hbm] * 8,
         out_specs=[hbm] * 4,
         scratch_shapes=[
             pltpu.VMEM(tall, bf),
@@ -593,6 +598,8 @@
             pltpu.VMEM(out_weight.shape, bf),
             pltpu.VMEM(conv_kernel.shape, bf),
             pltpu.VMEM(tall, bf),
+            pltpu.SMEM((pattern.shape[2], 1, frames), jnp.int32),
+            pltpu.SMEM(counts.shape, jnp.int32),
             pltpu.VMEM((SPAN, 2) + block, bf),
             pltpu.VMEM((SPAN,) + tall, bf),
             pltpu.VMEM((SPAN,) + tall, bf),
@@ -625,7 +632,7 @@
             pltpu.VMEM(tall, f32),
             pltpu.VMEM((2 * rows, width), f32),
             pltpu.VMEM((2 * rows, width), f32),
-            dma((6,)),
+            dma((8,)),
             dma((4,)),
         ]
         + [dma((SPAN,))] * 6

time: 58 us -> 57.2 us (0.986)
  Pallas kernels: 57 us -> 56.3 us
    pallas_call x1, Pallas kernels: 55.1 us -> 54.4 us  [on_device(): pl.pallas_call(partial(kernel, frames, heads), out_shape=shapes, in_specs...]
where the time goes in v5:
time: 57.2 us; the launch traced here: 57.1 us
  Pallas kernels  56.3 us (98%)
  between operations  0.8 us (1%)
    pallas_call x1, Pallas kernels, on_device(): pl.pallas_call(partial(kernel, frames, heads), out_shape=shapes, in_specs...  54.4 us
    pallas_call x1, Pallas kernels, on_device(): pl.pallas_call(copy_out, out_shape=shapes, in_specs=[vmem] * 4, out_specs...  1.91 us

profile of v5, /device:TPU:1, one launch (start us, length us, event | category | flops | bytes accessed | tf_op | source)
XLA Modules:
  0.0 57.1 jit_solution(16492675094327540650)
XLA Ops:
  0.6 54.4 %shard_map.111 = (bf16[128,512]{1,0:T(8,128)(2,1)}, bf16[512,128]{1,0:T(8,128)(2,1)}, bf16[512,128]{1,0:T(8,128)(2,1)}, bf16[512,128]{1,0:T(8,128)(2,1)}) custom-call(bf16[512,128]{1,0:T(8,128)(2,1)} %bitcast.9, bf16[512,128]{1,0:T(8,128)(2,1)} %bitcast.10, bf16[512,128]{1,0:T(8,128)(2,1)} %bitcast.11, bf16[128,1024]{1,0:T(8,128)(2,1)} %w_hbm.1, ...), custom_call_target="tpu_custom_call" | custom-call | tf_op jit(solution)/shard_map/pallas_call | solution.py:588
  55.0 1.9 %shard_map.112 = (bf16[128,512]{1,0:T(8,128)(2,1)}, bf16[512,128]{1,0:T(8,128)(2,1)}, bf16[512,128]{1,0:T(8,128)(2,1)}, bf16[512,128]{1,0:T(8,128)(2,1)}) custom-call(bf16[128,512]{1,0:T(8,128)(2,1)} %get-tuple-element.12.refs_0_, bf16[512,128]{1,0:T(8,128)(2,1)} %get-tuple-element.13.refs_1_, bf16[512,128]{1,0:T(8,128)(2,1)} %get-tuple-element.14.refs_2_, ...), custom_call_target="tpu_custom_call" | custom-call | tf_op jit(solution)/shard_map/pallas_call | solution.py:657

commit v6 on v5

--- a/solution.py
+++ b/solution.py
@@ -560,15 +560,17 @@
 
 
 def copy_out(*refs):
-    half = len(refs) // 2
-    sources, targets, sems = refs[:half], refs[half : 2 * half], refs[-1]
-    copies = [
-        pltpu.make_async_copy(src, dst, sems.at[n]) for n, (src, dst) in enumerate(zip(sources, targets))
-    ]
-    for copy in copies:
-        copy.start()
-    for copy in copies:
-        copy.wait()
+    sources, targets, held = refs[0:4], refs[4:8], refs[8:12]
+    in_sems, out_sems = refs[12:]
+    loads = [pltpu.make_async_copy(sources[n], held[n], in_sems.at[n]) for n in range(4)]
+    stores = [pltpu.make_async_copy(held[n], targets[n], out_sems.at[n]) for n in range(4)]
+    for load in loads:
+        load.start()
+    for load, store in zip(loads, stores):
+        load.wait()
+        store.start()
+    for store in stores:
+        store.wait()
 
 
 def on_device(queries, keys, values, out_weight, conv_kernel, grad_out, pattern, counts):
@@ -578,7 +580,6 @@
     block, tall = (rows, width), (width, rows)
     hbm = pl.BlockSpec(memory_space=pltpu.HBM)
     dma = pltpu.SemaphoreType.DMA
-    vmem = pl.BlockSpec(memory_space=pltpu.VMEM)
     shapes = [
         jax.ShapeDtypeStruct(tall, bf),
         jax.ShapeDtypeStruct(block, bf),
@@ -657,9 +658,9 @@
     conv_out, dq, dk, dv = pl.pallas_call(
         copy_out,
         out_shape=shapes,
-        in_specs=[vmem] * 4,
+        in_specs=[hbm] * 4,
         out_specs=[hbm] * 4,
-        scratch_shapes=[dma((4,))],
+        scratch_shapes=[pltpu.VMEM(shape.shape, bf) for shape in shapes] + [dma((4,)), dma((4,))],
     )(*results)
     return (
         conv_out.reshape(grad_out.shape),

time: 57.2 us -> 57.1 us (level)
  no operation moved by 1% of the time
where the time goes in v6:
time: 57.1 us; the launch traced here: 57 us
  Pallas kernels  56.2 us (98%)
  between operations  0.8 us (1%)
    pallas_call x1, Pallas kernels, on_device(): pl.pallas_call(partial(kernel, frames, heads), out_shape=shapes, in_specs...  54.4 us
    pallas_call x1, Pallas kernels, on_device(): pl.pallas_call(copy_out, out_shape=shapes, in_specs=[hbm] * 4, out_specs=...  1.82 us

profile of v6, /device:TPU:1, one launch (start us, length us, event | category | flops | bytes accessed | tf_op | source)
XLA Modules:
  0.0 57.0 jit_solution(9509458647241646762)
XLA Ops:
  0.6 54.4 %shard_map.111 = (bf16[128,512]{1,0:T(8,128)(2,1)}, bf16[512,128]{1,0:T(8,128)(2,1)}, bf16[512,128]{1,0:T(8,128)(2,1)}, bf16[512,128]{1,0:T(8,128)(2,1)}) custom-call(bf16[512,128]{1,0:T(8,128)(2,1)} %bitcast.9, bf16[512,128]{1,0:T(8,128)(2,1)} %bitcast.10, bf16[512,128]{1,0:T(8,128)(2,1)} %bitcast.11, bf16[128,1024]{1,0:T(8,128)(2,1)} %w_hbm.1, ...), custom_call_target="tpu_custom_call" | custom-call | tf_op jit(solution)/shard_map/pallas_call | solution.py:589
  55.0 1.8 %shard_map.112 = (bf16[128,512]{1,0:T(8,128)(2,1)}, bf16[512,128]{1,0:T(8,128)(2,1)}, bf16[512,128]{1,0:T(8,128)(2,1)}, bf16[512,128]{1,0:T(8,128)(2,1)}) custom-call(bf16[128,512]{1,0:T(8,128)(2,1)} %get-tuple-element.12.refs_0_, bf16[512,128]{1,0:T(8,128)(2,1)} %get-tuple-element.13.refs_1_, bf16[512,128]{1,0:T(8,128)(2,1)} %get-tuple-element.14.refs_2_, ...), custom_call_target="tpu_custom_call" | custom-call | tf_op jit(solution)/shard_map/pallas_call | solution.py:658
